TPU v7x, 256 devices: a whole 4x4x8 slice. The times are simulated.
256 devices in a mesh: wide: 64 (over y, z, core), narrow: 4 (over x).
Axes of the slice: x: 4, y: 4, z: 8, core: 2. Of those that a mesh axis runs over, the one named last changes fastest.
Arguments:
- left_edge: bfloat16 [448, 49, 448], P('wide', None, 'narrow'), may hold values from -40 to 40
- corner: bfloat16 [448, 448], P('narrow'), may hold values from -0.25 to 0.25
- right_edge: bfloat16 [448, 49, 448], P('wide', None, 'narrow'), may hold values from -0.25 to 0.25
- single_layer: bfloat16 [2, 2401], replicated, may hold values from -0.71875 to 0.71875
- warm_basis: bfloat16 [49, 448, 448], P(None, 'narrow', 'wide'), may hold values from -0.0390625 to 0.0390625
Outputs:
- new_basis: float32 [448, 49, 448], P('wide', None, 'narrow')
- r_factor: float32 [448, 448], replicated
All inputs are finite; a program needn't handle non-finite values.
Results may differ from a plain program's by a relative error of at most 0.014.
Values may be sent and summed in bfloat16 or wider, within the bound.
A program may use at most 128 MiB of HBM per device.

v0:
```python
import jax
import jax.numpy as jnp
from jax import lax
from jax.sharding import PartitionSpec as P

BOND = 7


def on_device(left_edge, corner, right_edge, single_layer, warm_basis):
    local_rows = left_edge.shape[0]
    square = left_edge.shape[1]
    breadth = corner.shape[1]
    local_cols = right_edge.shape[2]
    partial_value = jnp.dot(
        left_edge.reshape(local_rows * square, left_edge.shape[2]),
        corner,
        preferred_element_type=jnp.float32,
    )
    half_left = lax.psum(partial_value, "narrow").astype(jnp.bfloat16)
    layer = single_layer.astype(jnp.float32).reshape(single_layer.shape[0], BOND, BOND, BOND, BOND)
    piece = lax.all_gather(right_edge, "wide", axis=0, tiled=True)
    strip_sum = jnp.dot(
        half_left,
        piece.reshape(piece.shape[0], square * local_cols),
        preferred_element_type=jnp.float32,
    )
    strip = (
        strip_sum.astype(jnp.bfloat16)
        .astype(jnp.float32)
        .reshape(local_rows, BOND, BOND, BOND, BOND, local_cols)
    )
    ket_layer = jnp.einsum("iuvlmj,suldr->ivmsdrj", strip, layer)
    enlarged = jnp.einsum("ivmsdrj,svmew->iderwj", ket_layer, layer)
    enlarged = enlarged.astype(jnp.bfloat16).reshape(local_rows * square, square * local_cols)
    piece = lax.all_gather(warm_basis, "wide", axis=2, tiled=True)
    partial_rows = jnp.dot(
        enlarged,
        piece.reshape(square * local_cols, piece.shape[2]),
        preferred_element_type=jnp.float32,
    )
    projected = lax.psum(partial_rows.astype(jnp.bfloat16), "narrow").astype(jnp.float32)
    all_rows = breadth * square
    own_index = lax.axis_index("narrow")
    gram_term = (
        jnp.dot(
            projected.T,
            projected,
            precision=lax.Precision.HIGHEST,
            preferred_element_type=jnp.float32,
        )
        / all_rows
    )
    gram = lax.psum(gram_term, "wide")
    lower = jnp.linalg.cholesky(gram)
    solved = lax.linalg.triangular_solve(lower, projected.T, left_side=True, lower=True)
    own_solved = lax.dynamic_slice_in_dim(solved, own_index * local_cols, local_cols, 0)
    new_basis = own_solved.T.reshape(local_rows, square, local_cols)
    return (new_basis, lower.T)


def solution(mesh):
    placed = (
        P("wide", None, "narrow"),
        P("narrow", None),
        P("wide", None, "narrow"),
        P(),
        P(None, "narrow", "wide"),
    )
    return jax.shard_map(
        on_device,
        mesh=mesh,
        in_specs=placed,
        out_specs=(P("wide", None, "narrow"), P()),
        check_vma=False,
    )
```

profile of v0, /device:TPU:1, one launch (start us, length us, event | category | flops | bytes accessed | tf_op | source)
XLA Modules:
  0.0 571.7 jit_solution(11383188953171234222)
XLA Ops:
  7.2 0.7 all-gather.3.cloned.1.call-update
  8.0 1.6 copy.26
  9.6 0.9 reshape.65
  10.5 0.9 reshape.62
  11.5 0.3 fusion.47
  11.8 20.5 %all-reduce.10 = bf16[343,448]{0,1:T(8,128)(2,1)S(1)} all-reduce(f32[343,448]{0,1:T(8,128)S(1)} %fusion.47), channel_id=1, replica_groups=mesh['wide'=64,'narrow'=4] {'narrow'}, use_global_device_ids=true, to_apply=%region_0.0 | all-reduce | flops 153664 | bytes 921984 | tf_op jit(solution)/shard_map/psum | solution.py:19
  32.3 64.0 %all-gather.3.cloned.1.call-done = bf16[448,49,112]{2,1,0:T(8,128)(2,1)} async-done(((bf16[7,49,112]{2,1,0:T(8,128)(2,1)}), bf16[448,49,112]{2,1,0:T(8,128)(2,1)}) %all-gather.3.cloned.1.call-update) | async-done | bytes 4917264 | tf_op jit(solution)/shard_map/all_gather | solution.py:21
  96.3 11.7 %copy.20 = bf16[448,49,112]{0,2,1:T(8,128)(2,1)} copy(bf16[448,49,112]{2,1,0:T(8,128)(2,1)} %all-gather.3.cloned.1.call-done) | data formatting | bytes 9834496 | tf_op jit(solution)/shard_map/all_gather | solution.py:21
  108.0 7.0 %convolution_convert_fusion = bf16[343,5488]{1,0:T(8,128)(2,1)} fusion(bf16[448,5488]{0,1:T(8,128)(2,1)} %bitcast.85, bf16[343,448]{0,1:T(8,128)(2,1)S(1)} %all-reduce.10), kind=kOutput, calls=%fused_computation.5 | convolution fusion | flops 1688498432 | bytes 8989344 | tf_op jit(solution)/shard_map/dot_general | solution.py:22
  115.0 10.0 %reshape.64 = bf16[7,7,7,7,7,112]{5,4,3,2,1,0:T(8,128)(2,1)} reshape(bf16[343,5488]{1,0:T(8,128)(2,1)} %convolution_convert_fusion) | data formatting | bytes 7529536 | tf_op jit(solution)/shard_map/reshape | solution.py:30
  125.0 5.2 convolution_bitcast_fusion
  130.2 7.9 %fusion.2 = bf16[7,7,7,7,7,112]{5,4,2,3,1,0:T(8,128)(2,1)} fusion(bf16[7,7,7,2,7,7,112,1]{6,5,4,3,2,1,0,7:T(8,128)(2,1)S(1)} %convolution_bitcast_fusion, bf16[2,7,7,7,7,1,1,1]{4,3,2,1,0,7,6,5:T(8,128)(2,1)S(1)} %bitcast.89), kind=kOutput, calls=%fused_computation.7 | convolution fusion | flops 368947264 | bytes 11303908 | tf_op jit(solution)/shard_map/ivmsdrj,svmew->iderwj/dot_general | solution.py:33
  138.1 5.5 copy.25
  143.6 8.1 %reshape.66 = bf16[343,5488]{1,0:T(8,128)(2,1)} reshape(bf16[7,7,7,7,7,112]{5,4,3,2,1,0:T(8,128)(2,1)} %copy.25) | data formatting | bytes 7529536 | tf_op jit(solution)/shard_map/reshape | solution.py:34
  151.7 25.8 %all-gather.5.cloned.1.call-done = bf16[49,112,448]{1,0,2:T(8,128)(2,1)} async-done(((bf16[49,112,7]{1,0,2:T(8,128)(2,1)}), bf16[49,112,448]{1,0,2:T(8,128)(2,1)}) %all-gather.5.cloned.1.call-update) | async-done | bytes 4917264 | tf_op jit(solution)/shard_map/all_gather | solution.py:35
  177.5 11.6 %copy.27 = bf16[49,112,448]{2,1,0:T(8,128)(2,1)} copy(bf16[49,112,448]{1,0,2:T(8,128)(2,1)} %all-gather.5.cloned.1.call-done) | data formatting | bytes 9834496 | tf_op jit(solution)/shard_map/all_gather | solution.py:35
  189.1 7.3 %convolution_convert_fusion.1 = bf16[343,448]{0,1:T(8,128)(2,1)} fusion(bf16[343,5488]{1,0:T(8,128)(2,1)} %reshape.66, bf16[5488,448]{1,0:T(8,128)(2,1)} %bitcast.86), kind=kOutput, calls=%fused_computation.10 | convolution fusion | flops 1686769664 | bytes 8989344 | tf_op jit(solution)/shard_map/dot_general | solution.py:36
  196.4 0.3 all-reduce.9.cloned.1.call-start
  196.6 41.0 %all-reduce.7.cloned.1.call-done = bf16[343,448]{0,1:T(8,128)(2,1)} async-done(((bf16[343,448]{0,1:T(8,128)(2,1)}), bf16[343,448]{0,1:T(8,128)(2,1)}) %all-reduce.7.cloned.1.call-update) | async-done | bytes 307344 | tf_op jit(solution)/shard_map/psum | solution.py:41
  237.7 2.4 convolution_multiply_fusion
  240.1 0.6 iota_multiply_fusion
  240.7 0.6 pad_convert_fusion
  241.4 1.0 bitcast_convert_fusion.1
  242.4 185.3 %all-reduce.9.cloned.1.call-done = f32[448,448]{0,1:T(8,128)} async-done(((f32[448,448]{0,1:T(8,128)}), f32[448,448]{0,1:T(8,128)}) %all-reduce.9.cloned.1.call-update) | async-done | bytes 802832 | tf_op jit(solution)/shard_map/psum | solution.py:53
  427.7 1.5 copy.29
  429.2 1.4 fusion.6
  430.6 11.7 %cholesky.105 = f32[128,128]{1,0:T(8,128)S(1)} custom-call(f32[128,128]{1,0:T(8,128)S(1)} %cholesky.272), custom_call_target="Cholesky" | custom-call | tf_op jit(solution)/shard_map/jit(cholesky)/cholesky | solution.py:54
  442.3 9.8 %custom-call.30 = f32[1,128,128]{1,2,0:T(8,128)S(1)} custom-call(f32[1,128,128]{2,1,0:T(8,128)S(1)} %get-tuple-element.35), custom_call_target="InvertDiagBlocksLowerTriangular" | custom-call | tf_op jit(solution)/shard_map/jit(cholesky)/cholesky | solution.py:54
  452.3 0.3 constant_dynamic-update-slice_fusion
  452.6 0.3 convolution_subtract_fusion.2
  452.9 11.7 %cholesky.219 = f32[128,128]{1,0:T(8,128)S(1)} custom-call(f32[128,128]{1,0:T(8,128)S(1)} %cholesky.276), custom_call_target="Cholesky" | custom-call | tf_op jit(solution)/shard_map/jit(cholesky)/cholesky | solution.py:54
  464.6 10.2 %custom-call.31 = f32[1,128,128]{1,2,0:T(8,128)S(1)} custom-call(f32[1,128,128]{2,1,0:T(8,128)S(1)} %get-tuple-element.32), custom_call_target="InvertDiagBlocksLowerTriangular" | custom-call | tf_op jit(solution)/shard_map/jit(cholesky)/cholesky | solution.py:54
  474.8 0.2 convolution_dynamic-update-slice_fusion
  475.1 0.3 convolution_subtract_fusion.3
  475.4 11.7 %cholesky.240 = f32[128,128]{1,0:T(8,128)S(1)} custom-call(f32[128,128]{1,0:T(8,128)S(1)} %cholesky.281), custom_call_target="Cholesky" | custom-call | tf_op jit(solution)/shard_map/jit(cholesky)/cholesky | solution.py:54
  487.2 0.6 compare_reduce_fusion.1
  487.8 9.8 %custom-call.32 = f32[1,128,128]{1,2,0:T(8,128)S(1)} custom-call(f32[1,128,128]{2,1,0:T(8,128)S(1)} %get-tuple-element.29), custom_call_target="InvertDiagBlocksLowerTriangular" | custom-call | tf_op jit(solution)/shard_map/jit(cholesky)/cholesky | solution.py:54
  497.6 0.2 convolution_dynamic-update-slice_fusion.1
  497.8 0.2 convolution_subtract_fusion.5
  498.1 5.8 %cholesky.260 = f32[64,64]{1,0:T(8,128)S(1)} custom-call(f32[64,64]{1,0:T(8,128)S(1)} %convolution_subtract_fusion.5), custom_call_target="Cholesky" | custom-call | tf_op jit(solution)/shard_map/jit(cholesky)/cholesky | solution.py:54
  503.9 0.7 compare_reduce_fusion
  504.7 0.7 compare_reduce_fusion.2
  508.0 0.2 fusion.8
  508.2 0.7 triangular_solve.109
  508.9 8.4 %while.1 = (s32[]{:T(128)}, f32[448,448]{1,0:T(8,128)S(1)}, s32[3,2]{0,1:T(2,128)S(1)}, f32[3,128,128]{2,1,0:T(8,128)}, s32[]{:T(128)}) while((s32[]{:T(128)}, f32[448,448]{1,0:T(8,128)S(1)}, s32[3,2]{0,1:T(2,128)S(1)}, f32[3,128,128]{2,1,0:T(8,128)}, s32[]{:T(128)}) %tuple.35), condition=%wide.while_cond, body=%wide.while_body.sunk | while | flops 2 | bytes 132705 | solution.py:55
  509.1 0.6 fusion.62
  509.7 2.1 bitcast_dynamic-update-slice_fusion.2
  511.9 0.6 fusion.62
  512.5 2.1 bitcast_dynamic-update-slice_fusion.2
  514.6 0.6 fusion.62
  515.2 2.1 bitcast_dynamic-update-slice_fusion.2
  517.2 0.9 fusion.37
  518.2 0.9 pad_maximum_fusion
  519.1 39.3 %custom-call.33 = f32[4,128,128]{1,2,0:T(8,128)S(1)} custom-call(f32[4,128,128]{2,1,0:T(8,128)S(1)} %pad_maximum_fusion), custom_call_target="InvertDiagBlocksLowerTriangular" | custom-call | tf_op jit(solution)/shard_map/triangular_solve | solution.py:55
  558.5 1.2 fusion.30
  559.7 0.3 convolution_subtract_fusion.1
  560.0 0.5 fusion.36
  560.6 0.5 convolution_subtract_fusion
  561.1 0.5 fusion.34
  561.6 0.6 convolution_subtract_fusion.4
  562.3 0.5 fusion.42
  562.8 0.3 fusion.24
  563.0 0.7 reshape.68
  563.7 1.2 copy.33
  (24 shorter events, 0.7 us)
Async XLA Ops:
  7.2 4.3 copy-start
  7.2 89.1 %all-gather.3.cloned.1.call-start = ((), (), s32[]{:S(2)}) async-start(), calls=%async_computation | async-start | bytes 6522880 | tf_op jit(solution)/shard_map/all_gather | solution.py:21
  7.9 169.6 %all-gather.5.cloned.1.call-start = ((), (), s32[]{:S(2)}) async-start(), calls=%async_computation.1 | async-start | bytes 6522880 | tf_op jit(solution)/shard_map/all_gather | solution.py:35
  9.5 228.1 %all-reduce.7.cloned.1.call-start = ((), (), s32[]{:S(2)}) async-start(), calls=%async_computation.2 | async-start | bytes 688128 | tf_op jit(solution)/shard_map/psum | solution.py:41
  196.4 231.3 %all-reduce.9.cloned.1.call-start = ((), (), s32[]{:S(2)}) async-start(), calls=%async_computation.3 | async-start | bytes 1835008 | tf_op jit(solution)/shard_map/psum | solution.py:53
  508.0 57.0 %copy-start.1 = (bf16[112,448]{1,0:T(8,128)(2,1)S(1)}, bf16[112,448]{1,0:T(8,128)(2,1)}, u32[]{:S(2)}) copy-start(bf16[112,448]{1,0:T(8,128)(2,1)} %param.6) | copy-start | bytes 301060
Sparse Core Ops, SparseCore 0:
  10.7 85.5 all-gather.2
  99.5 77.8 all-gather.4
  196.5 41.1 all-reduce.6
  241.5 186.1 all-reduce.8
where the time goes:
time: 579 us; the launch traced here: 572 us
  waiting for transfers between devices  317 us (55%)
  other arithmetic  118 us (20%)
  local copies, waits for them, and re-layouts  62.7 us (11%)
  matrix products  36 us (6%)
  blocking collectives  20.5 us (4%)
  between operations  16.8 us (3%)
    psum x1, waiting for transfers between devices, on_device(): gram = lax.psum(gram_term, 'wide')  185 us
    another operation x14, other arithmetic, on_device(): lower = jnp.linalg.cholesky(gram)  73 us
    all_gather x1, waiting for transfers between devices, on_device(): piece = lax.all_gather(right_edge, 'wide', axis=0, tiled=True)  64 us
    another operation x6, other arithmetic, on_device(): lax.linalg.triangular_solve(lower, projected.T, left_side=True, lower=True)  42.4 us
    psum x1, waiting for transfers between devices, on_device(): lax.psum(partial_rows.astype(jnp.bfloat16), 'narrow').astype(jnp.float32)  41 us
    all_gather x1, waiting for transfers between devices, on_device(): piece = lax.all_gather(warm_basis, 'wide', axis=2, tiled=True)  25.8 us
    psum x1, blocking collectives, on_device(): half_left = lax.psum(partial_value, 'narrow').astype(jnp.bfloat16)  20.5 us
    all_gather x1, local copies, waits for them, and re-layouts, on_device(): piece = lax.all_gather(right_edge, 'wide', axis=0, tiled=True)  11.7 us
  transfers between devices with their start and end apart: 4, of which 4 were waited for; matrix products, arithmetic and copies ran while one was open for 11% of the time, Pallas kernels for 0%

commit v1 on v0

v1 whole, which is shorter than its diff:
```python
import functools

import jax
import jax.numpy as jnp
from jax import lax
from jax.experimental import pallas as pl
from jax.experimental.pallas import tpu as pltpu
from jax.sharding import PartitionSpec as P

BOND = 7
BLOCK = 64
SLOT = 16
HALF = 3200
A_LANES = 1280
ROWS = 400
HI = lax.Precision.HIGHEST
MESH = pl.DeviceIdType.MESH
MIB = 1 << 20


def place():
    wide = lax.axis_index("wide")
    core = lax.rem(wide, 2)
    z = lax.rem(lax.div(wide, 2), 8)
    y = lax.div(wide, 16)
    return y, z, core, lax.axis_index("narrow")


def wide_of(y, z, core):
    return (y * 8 + z) * 2 + core


def greet(peers):
    barrier = pltpu.get_barrier_semaphore()
    for peer in peers:
        pl.semaphore_signal(barrier, inc=1, device_id=peer, device_id_type=MESH)
    pl.semaphore_wait(barrier, len(peers))


def gather_kernel(right, warm, left, corner, right_all, warm_all, left_all, corner_all,
                  paired, merged, pair_s, pair_r, own_s, ring_r, near_s, far_s, yl_s, ys_s, first_s,
                  part_s, part_r, x_s, x_r):
    y, z, core, x = place()
    zdir = 1 - 2 * core

    def zmove(k):
        return lax.rem(z + 8 + k * zdir, 8)

    def ymove(k):
        return lax.rem(y + 4 + k * zdir, 4)

    def at(yy, zz, cc=None):
        return (wide_of(yy, zz, core if cc is None else cc), x)

    partner = at(y, z, 1 - core)
    peers = [partner, at(y, zmove(1)), at(y, zmove(-1)), at(ymove(1), z), at(ymove(2), z), at(ymove(3), z)]
    peers += [(wide_of(y, z, core), lax.rem(x + d, 4)) for d in (1, 2, 3)]
    greet(peers)

    pending = []

    def push(src, dst, ss, rs, device):
        c = pltpu.make_async_remote_copy(src_ref=src, dst_ref=dst, send_sem=ss, recv_sem=rs,
                                         device_id=device, device_id_type=MESH)
        c.start()
        pending.append(c)

    arrays = ((right, right_all), (warm, warm_all))
    pairs = []
    for g, (src, _) in enumerate(arrays):
        c = pltpu.make_async_remote_copy(src_ref=src.at[1 - core], dst_ref=paired.at[g], send_sem=pair_s.at[g],
                                         recv_sem=pair_r.at[g], device_id=partner, device_id_type=MESH)
        c.start()
        pairs.append(c)
    xcopies = []
    for src, dst, k in ((left, left_all, 0), (corner, corner_all, 1)):
        for d in (1, 2, 3):
            c = pltpu.make_async_remote_copy(
                src_ref=src, dst_ref=dst.at[x], send_sem=x_s.at[k, d - 1], recv_sem=x_r.at[k, d - 1],
                device_id=(wide_of(y, z, core), lax.rem(x + d, 4)), device_id_type=MESH)
            c.start()
            xcopies.append(c)
    own_x = []
    for src, dst, k in ((left, left_all, 0), (corner, corner_all, 1)):
        c = pltpu.make_async_copy(src, dst.at[x], own_s.at[2 + k])
        c.start()
        own_x.append(c)

    bounds = ((0, A_LANES), (A_LANES, HALF))

    def view(g, half, part, yy, zz):
        lo, hi = bounds[part]
        rows = pl.ds(pl.multiple_of((yy * 8 + zz) * SLOT, SLOT), SLOT)
        return arrays[g][1].at[half, rows, lo:hi]

    def slot(yy, zz):
        return yy * 8 + zz

    def send(g, part, yy, zz, sem, device, src=None):
        v = view(g, core, part, yy, zz)
        push(v if src is None else src, v, sem.at[g, part, slot(yy, zz)], ring_r.at[g, part, slot(yy, zz)], device)

    def forward_partner(g, part, yy, zz, src=None):
        v = view(g, core, part, yy, zz)
        push(v if src is None else src, v, part_s.at[g, part, slot(yy, zz)], part_r.at[g, part, slot(yy, zz)], partner)

    def arrived(g, part, yy, zz):
        v = view(g, core, part, yy, zz)
        pltpu.make_async_copy(v, v, ring_r.at[g, part, slot(yy, zz)]).wait()

    own_copies = []
    znext, zprev = at(y, zmove(1)), at(y, zmove(-1))
    ynext, yprev = at(ymove(1), z), at(ymove(-1), z)

    def begin(g):
        pairs[g].wait()
        merged[g] = paired[g] + arrays[g][0][core]
        c = pltpu.make_async_copy(
            merged.at[g], arrays[g][1].at[core, pl.ds(pl.multiple_of((y * 8 + z) * SLOT, SLOT), SLOT), :], own_s.at[g])
        c.start()
        own_copies.append(c)
        a, b = merged.at[g, :, 0:A_LANES], merged.at[g, :, A_LANES:HALF]
        va = view(g, core, 0, y, z)
        for d in (1, 2, 3):
            push(a, va, first_s.at[g, d - 1], ring_r.at[g, 0, slot(y, z)], at(ymove(d), z))
        send(g, 1, y, z, near_s, znext, b)
        send(g, 1, y, z, far_s, zprev, b)
        send(g, 0, y, z, near_s, znext, a)
        send(g, 0, y, z, far_s, zprev, a)
        send(g, 1, y, z, yl_s, ynext, b)
        send(g, 1, y, z, ys_s, yprev, b)
        forward_partner(g, 0, y, z, a)
        forward_partner(g, 1, y, z, b)

    def column(g):
        for d in (1, 2, 3):
            yy = ymove(d)
            arrived(g, 0, yy, z)
            send(g, 0, yy, z, near_s, znext)
            send(g, 0, yy, z, far_s, zprev)
            forward_partner(g, 0, yy, z)

    def b_ring(g, s, way):
        zz = zmove(-s) if way > 0 else zmove(s)
        arrived(g, 1, y, zz)
        if way > 0 and s < 4:
            send(g, 1, y, zz, near_s, znext)
        if way < 0 and s < 3:
            send(g, 1, y, zz, far_s, zprev)
        send(g, 1, y, zz, yl_s, ynext)
        send(g, 1, y, zz, ys_s, yprev)
        forward_partner(g, 1, y, zz)

    def a_ring(g, s, way, d):
        zz = zmove(-s) if way > 0 else zmove(s)
        yy = ymove(d)
        arrived(g, 0, yy, zz)
        if way > 0 and s < 4:
            send(g, 0, yy, zz, near_s, znext)
        if way < 0 and s < 3:
            send(g, 0, yy, zz, far_s, zprev)
        forward_partner(g, 0, yy, zz)

    def y_pass(g, zz):
        arrived(g, 1, ymove(-1), zz)
        send(g, 1, ymove(-1), zz, yl_s, ynext)
        forward_partner(g, 1, ymove(-1), zz)
        arrived(g, 1, ymove(1), zz)
        forward_partner(g, 1, ymove(1), zz)

    def y_last(g, zz):
        arrived(g, 1, ymove(2), zz)
        forward_partner(g, 1, ymove(2), zz)

    def ring(g):
        y_pass(g, z)
        for s in (1, 2, 3, 4):
            for way in (1, -1):
                if way < 0 and s == 4:
                    continue
                b_ring(g, s, way)
                for d in range(4):
                    a_ring(g, s, way, d)
            if s > 1:
                y_pass(g, zmove(-(s - 1)))
                y_pass(g, zmove(s - 1))

    def finish(g):
        y_pass(g, zmove(-4))
        for k in range(8):
            y_last(g, zmove(k))

    for g in (0, 1):
        begin(g)
    for g in (0, 1):
        column(g)
    for g in (0, 1):
        ring(g)
    for g in (0, 1):
        finish(g)
    for g in (0, 1):
        for part in (0, 1):
            for s in range(32):
                v = view(g, 1 - core, part, s // 8, s % 8)
                pltpu.make_async_copy(v, v, part_r.at[g, part, s]).wait()
    for c in pending:
        c.wait_send()
    for c in xcopies:
        c.wait()
    for c in own_copies + own_x:
        c.wait()


def gathers(right, warm, left, corner):
    dma = pltpu.SemaphoreType.DMA
    any_ = pl.BlockSpec(memory_space=pl.ANY)
    vm = pl.BlockSpec(memory_space=pltpu.VMEM)
    return pl.pallas_call(
        gather_kernel,
        out_shape=[
            jax.ShapeDtypeStruct((2, 32 * SLOT, HALF), jnp.bfloat16),
            jax.ShapeDtypeStruct((2, 32 * SLOT, HALF), jnp.bfloat16),
            jax.ShapeDtypeStruct((4, ROWS, 128), jnp.bfloat16),
            jax.ShapeDtypeStruct((4, 128, 512), jnp.bfloat16),
        ],
        in_specs=[vm] * 4,
        out_specs=[any_] * 4,
        scratch_shapes=[
            pltpu.VMEM((2, SLOT, HALF), jnp.bfloat16),
            pltpu.VMEM((2, SLOT, HALF), jnp.bfloat16),
            dma((2,)), dma((2,)), dma((4,)), dma((2, 2, 32)), dma((2, 2, 32)), dma((2, 2, 32)),
            dma((2, 2, 32)), dma((2, 2, 32)), dma((2, 3)), dma((2, 2, 32)), dma((2, 2, 32)), dma((2, 3)), dma((2, 3)),
        ],
        compiler_params=pltpu.CompilerParams(collective_id=1, has_side_effects=True, vmem_limit_bytes=48 * MIB),
        name="gathers",
    )(right, warm, left, corner)


def contract_kernel(right, warm, left, corner, ket, bra, pick, out, half, strip, layered, enlarged, total):
    acc = jnp.zeros((ROWS, 512), jnp.float32)
    for n in range(4):
        acc += jnp.dot(left[n], corner[n], preferred_element_type=jnp.float32)
    half[...] = acc.astype(jnp.bfloat16)

    for h in range(2):
        @pl.loop(0, 5)
        def _(chunk):
            cols = pl.ds(pl.multiple_of(chunk * 640, 640), 640)
            res = jnp.dot(half[...], right[h, :, cols], preferred_element_type=jnp.float32)
            for j in range(5):
                rows = pl.ds(pl.multiple_of((h * 25 + chunk * 5 + j) * 8, 8), 8)
                strip[:, rows, :] = res[:, j * 128:(j + 1) * 128].reshape(50, 8, 128)

    @pl.loop(0, 25)
    def _(t):
        x = jnp.concatenate([strip[2 * t].astype(jnp.bfloat16), strip[2 * t + 1].astype(jnp.bfloat16)], axis=1)
        res = jnp.dot(ket[...], x, preferred_element_type=jnp.float32).astype(jnp.bfloat16)
        for j in range(2):
            rows = pl.ds(pl.multiple_of((2 * t + j) * 16, 16), 16)
            layered[:, rows, :] = res[:, j * 128:(j + 1) * 128].reshape(49, 16, 128)

    enlarged[49] = jnp.zeros((ROWS, 128), jnp.float32)

    @pl.loop(0, 50)
    def _(b):
        enlarged[b, 392:400, :] = jnp.zeros((8, 128), jnp.float32)

    @pl.loop(0, 49)
    def _(dr):
        d, r = lax.div(dr, 7), lax.rem(dr, 7)
        x = jnp.concatenate([layered[dr, i * 112:(i + 1) * 112, :] for i in range(7)], axis=1)
        res = jnp.dot(bra[...], x, preferred_element_type=jnp.float32)
        for i in range(7):
            rows = pl.ds(pl.multiple_of((i * 7 + d) * 8, 8), 8)
            for s in range(7):
                enlarged[r * 7 + s, rows, :] = res[s * 8:(s + 1) * 8, i * 128:(i + 1) * 128]

    total[...] = jnp.zeros_like(total)
    for h in range(2):
        @pl.loop(0, 5)
        def _(chunk):
            cols = pl.ds(pl.multiple_of(chunk * 640, 640), 640)
            x = jnp.concatenate(
                [enlarged[h * 25 + chunk * 5 + j].astype(jnp.bfloat16) for j in range(5)], axis=1)
            total[...] += lax.dot_general(x, warm[h, :, cols], (((1,), (1,)), ((), ())),
                                          preferred_element_type=jnp.float32)
    res = jnp.dot(total[...].astype(jnp.bfloat16), pick[...], preferred_element_type=jnp.float32)
    for n in range(4):
        out[n] = res[:, n * 128:(n + 1) * 128].astype(jnp.bfloat16)


def contract(right, warm, left, corner, ket, bra, pick):
    vm = pl.BlockSpec(memory_space=pltpu.VMEM)
    return pl.pallas_call(
        contract_kernel,
        out_shape=jax.ShapeDtypeStruct((4, ROWS, 128), jnp.bfloat16),
        in_specs=[vm] * 7,
        out_specs=vm,
        scratch_shapes=[
            pltpu.VMEM((ROWS, 512), jnp.bfloat16),
            pltpu.VMEM((50, ROWS, 128), jnp.float32),
            pltpu.VMEM((49, 800, 128), jnp.bfloat16),
            pltpu.VMEM((50, ROWS, 128), jnp.float32),
            pltpu.VMEM((ROWS, 512), jnp.float32),
        ],
        compiler_params=pltpu.CompilerParams(vmem_limit_bytes=60 * MIB),
        name="contract",
    )(right, warm, left, corner, ket, bra, pick)


def sums_kernel(part, proj, gram, got, slab, got1, piece, got2, n_s, n_r, p_s, p_r, a_s, a_r, b_s, b_r,
                c_s, c_r, d_s, d_r, e_s, e_r, f_s, f_r):
    y, z, core, x = place()
    others = [(lax.rem(y + k // 2, 4), lax.rem(core + k % 2, 2)) for k in range(1, 8)]
    xs = [lax.rem(x + d, 4) for d in (1, 2, 3)]
    zs = [lax.rem(z + d, 8) for d in range(1, 8)]
    me = wide_of(y, z, core)
    greet([(me, xx) for xx in xs] + [(wide_of(yy, z, cc), x) for yy, cc in others]
          + [(wide_of(y, zz, core), x) for zz in zs])

    def start(src, dst, ss, rs, device):
        c = pltpu.make_async_remote_copy(src_ref=src, dst_ref=dst, send_sem=ss, recv_sem=rs,
                                         device_id=device, device_id_type=MESH)
        c.start()
        return c

    c1 = [start(part.at[xs[d]], got.at[d], n_s.at[d], n_r.at[d], (me, xs[d])) for d in range(3)]
    acc = part[x].astype(jnp.float32)
    for d in range(3):
        c1[d].wait_recv()
        acc += got[d].astype(jnp.float32)
    proj[x] = acc.astype(jnp.bfloat16)
    c2 = [start(proj.at[x], proj.at[x], p_s.at[d], p_r.at[d], (me, xs[d])) for d in range(3)]
    own = acc.astype(jnp.bfloat16)
    tn = (((0,), (0,)), ((), ()))
    scale = 1.0 / (448 * 49)

    def product(n):
        slab[pl.ds(pl.multiple_of(n * 128, 128), 128), :] = lax.dot_general(
            proj[n], own, tn, preferred_element_type=jnp.float32) * scale

    product(x)
    for d in (0, 2, 1):
        c2[d].wait_recv()
        product(lax.rem(x + 3 - d, 4))

    def rows(k, size):
        return pl.ds(pl.multiple_of(k * size, size), size)

    mine = y * 2 + core
    c3 = [start(slab.at[rows(yy * 2 + cc, 64)], got1.at[k], a_s.at[k], a_r.at[k], (wide_of(yy, z, cc), x))
          for k, (yy, cc) in enumerate(others)]
    acc = slab[rows(mine, 64), :]
    for k in range(7):
        c3[k].wait_recv()
        acc += got1[k]
    piece[...] = acc
    c4 = [start(piece.at[rows(zz, 8)], got2.at[k], b_s.at[k], b_r.at[k], (wide_of(y, zz, core), x))
          for k, zz in enumerate(zs)]
    acc = piece[rows(z, 8), :]
    for k in range(7):
        c4[k].wait_recv()
        acc += got2[k]
    spot = gram.at[x, y, core, rows(z, 8)]
    gram[x, y, core, rows(z, 8), :] = acc
    c5 = [start(spot, spot, c_s.at[k], c_r.at[k], (wide_of(y, zz, core), x)) for k, zz in enumerate(zs)]
    for c in c5:
        c.wait_recv()
    spot = gram.at[x, y, core]
    c6 = [start(spot, spot, d_s.at[d], d_r.at[d], (me, xs[d])) for d in range(3)]
    for c in c6:
        c.wait_recv()
    spot = gram.at[:, y, core]
    c7 = [start(spot, spot, e_s.at[d - 1], e_r.at[d - 1], (wide_of(lax.rem(y + d, 4), z, core), x)) for d in (1, 2, 3)]
    other = (wide_of(y, z, 1 - core), x)
    c8 = [start(spot, spot, f_s.at[0], f_r.at[0], other)]
    for d in (3, 1, 2):
        c7[d - 1].wait_recv()
        spot = gram.at[:, lax.rem(y + 4 - d, 4), core]
        c8.append(start(spot, spot, f_s.at[d], f_r.at[d], other))
    for c in c8:
        c.wait()
    for c in c1 + c2 + c3 + c4 + c5 + c6 + c7:
        c.wait_send()


def sums(part):
    dma = pltpu.SemaphoreType.DMA
    vm = pl.BlockSpec(memory_space=pltpu.VMEM)
    return pl.pallas_call(
        sums_kernel,
        out_shape=[
            jax.ShapeDtypeStruct((4, ROWS, 128), jnp.bfloat16),
            jax.ShapeDtypeStruct((4, 4, 2, 64, 128), jnp.float32),
        ],
        in_specs=[vm],
        out_specs=[vm, vm],
        scratch_shapes=[
            pltpu.VMEM((3, ROWS, 128), jnp.bfloat16),
            pltpu.VMEM((512, 128), jnp.float32),
            pltpu.VMEM((7, 64, 128), jnp.float32),
            pltpu.VMEM((64, 128), jnp.float32),
            pltpu.VMEM((7, 8, 128), jnp.float32),
            dma((3,)), dma((3,)), dma((3,)), dma((3,)), dma((7,)), dma((7,)), dma((7,)), dma((7,)),
            dma((7,)), dma((7,)), dma((3,)), dma((3,)), dma((3,)), dma((3,)), dma((4,)), dma((4,)),
        ],
        compiler_params=pltpu.CompilerParams(collective_id=2, has_side_effects=True, vmem_limit_bytes=32 * MIB),
        name="sums",
    )(part)


def eliminate(diag):
    n = BLOCK
    row_id = lax.broadcasted_iota(jnp.int32, (n, n), 0)
    col_id = lax.broadcasted_iota(jnp.int32, (n, n), 1)
    eye = jnp.where(row_id == col_id, 1.0, 0.0).astype(jnp.float32)
    wide = jnp.concatenate([diag, eye], axis=1)
    groups = [wide[8 * g:8 * g + 8] for g in range(n // 8)]
    sub = lax.broadcasted_iota(jnp.int32, (8, 2 * n), 0)
    for k in range(n):
        g, t = divmod(k, 8)
        pivot = groups[g][t:t + 1, :]
        scaled = pivot * (1.0 / pivot[:, k:k + 1])
        for h in range(g, n // 8):
            if h == g and t == 7:
                continue
            update = groups[h][:, k:k + 1] * scaled
            if h == g:
                update = jnp.where(sub > t, update, 0.0)
            groups[h] = groups[h] - update
    wide = jnp.concatenate(groups, axis=0)
    upper, lower = wide[:, :n], wide[:, n:]
    d = jnp.sum(upper * eye, axis=1, keepdims=True)
    root = lax.rsqrt(d)
    root = root * (1.5 - 0.5 * d * root * root)
    return jnp.where(row_id <= col_id, upper * root, 0.0), jnp.where(row_id >= col_id, lower * root, 0.0)


def factor_kernel(gram, proj, r_ref, out, work):
    n = 448
    x = lax.axis_index("narrow")
    for a in range(4):
        for b in range(4):
            work[a * 112:(a + 1) * 112, b * 112:(b + 1) * 112] = gram[b, a * 128:a * 128 + 112, 0:112]
    r_ref[...] = jnp.zeros_like(r_ref)
    col = lax.broadcasted_iota(jnp.int32, (BLOCK, n), 1)
    row = lax.broadcasted_iota(jnp.int32, (BLOCK, n), 0)
    for b in range(n // BLOCK):
        lo, hi = b * BLOCK, (b + 1) * BLOCK
        r, inverse = eliminate(work[lo:hi, lo:hi])
        inside = (col >= lo) & (col < hi)
        src = jnp.where(inside, jnp.where(col - lo == row, 1.0, 0.0), work[lo:hi, :])
        full = jnp.dot(inverse, src, precision=HI, preferred_element_type=jnp.float32)
        work[lo:hi, :] = jnp.where(col < hi, full, 0.0)
        rest = jnp.where(col >= hi, full, 0.0)
        r_ref[lo:hi, :] = rest
        r_ref[lo:hi, lo:hi] = r
        if hi < n:
            at = lax.broadcasted_iota(jnp.int32, (n - hi, n), 1)
            old = jnp.where((at >= lo) & (at < hi), 0.0, work[hi:, :])
            work[hi:, :] = old - lax.dot_general(rest[:, hi:], full, (((0,), (0,)), ((), ())), precision=HI,
                                                 preferred_element_type=jnp.float32)
    own = work[pl.ds(pl.multiple_of(x * 112, 8), 112), :]
    nt = (((1,), (1,)), ((), ()))
    acc = jnp.zeros((ROWS, 112), jnp.float32)
    for b in range(4):
        acc += lax.dot_general(proj[b][:, 0:112].astype(jnp.float32), own[:, b * 112:(b + 1) * 112], nt, precision=HI,
                               preferred_element_type=jnp.float32)
    out[...] = acc


def factor(gram, proj):
    vm = pl.BlockSpec(memory_space=pltpu.VMEM)
    return pl.pallas_call(
        factor_kernel,
        out_shape=[jax.ShapeDtypeStruct((448, 448), jnp.float32), jax.ShapeDtypeStruct((ROWS, 112), jnp.float32)],
        in_specs=[vm, vm],
        out_specs=[vm, vm],
        scratch_shapes=[pltpu.VMEM((448, 448), jnp.float32)],
        compiler_params=pltpu.CompilerParams(vmem_limit_bytes=40 * MIB),
        name="factor",
    )(gram, proj)


def shard_rows(block, core):
    rows = jnp.pad(block, ((0, 0), (0, 1), (0, 16))).reshape(7, 2, HALF).transpose(1, 0, 2)
    return jnp.where(core == 0, jnp.pad(rows, ((0, 0), (0, 9), (0, 0))), jnp.pad(rows, ((0, 0), (7, 2), (0, 0))))


def layers(single_layer):
    layer = single_layer.reshape(2, BOND, BOND, BOND, BOND)
    eye = jnp.eye(BOND, dtype=layer.dtype)
    ket = jnp.einsum("suldr,mn->drsmlnu", layer, eye)
    ket = jnp.pad(ket.reshape(49, 14, 49, 7), ((0, 0), (0, 2), (0, 1), (0, 1))).reshape(784, ROWS)
    bra = layer.transpose(4, 3, 1, 0, 2).reshape(7, 7, 7, 14)
    bra = jnp.pad(bra, ((0, 0), (0, 1), (0, 0), (0, 2))).reshape(56, 112)
    return ket, bra


def picker():
    at = lax.broadcasted_iota(jnp.int32, (512, 512), 0)
    to = lax.broadcasted_iota(jnp.int32, (512, 512), 1)
    held = jnp.where(at % 16 < 14, at // 16 * 14 + at % 16, -1)
    wanted = jnp.where(to % 128 < 112, to // 128 * 112 + to % 128, -2)
    return (held == wanted).astype(jnp.bfloat16)


def on_device(left_edge, corner, right_edge, single_layer, warm_basis):
    core = lax.axis_index("wide") % 2
    right = shard_rows(right_edge, core)
    warm = shard_rows(warm_basis.transpose(2, 0, 1), core)
    left = left_edge.reshape(7, 7, 7, 112).transpose(0, 2, 1, 3)
    left = jnp.pad(left, ((0, 0), (0, 0), (0, 1), (0, 16))).reshape(392, 128)
    left = jnp.pad(left, ((0, 8), (0, 0)))
    corner = jnp.pad(corner.reshape(112, 32, 14), ((0, 16), (0, 0), (0, 2))).reshape(128, 512)
    ket, bra = layers(single_layer)
    right, warm, left, corner = gathers(right, warm, left, corner)
    part = contract(right, warm, left, corner, ket, bra, picker())
    proj, gram = sums(part)
    r_factor, rows = factor(gram.reshape(4, 512, 128), proj)
    new_basis = rows[:392].reshape(7, 7, 8, 112)[:, :, :7].reshape(7, 49, 112)
    return new_basis, r_factor


def solution(mesh):
    placed = (
        P("wide", None, "narrow"),
        P("narrow", None),
        P("wide", None, "narrow"),
        P(),
        P(None, "narrow", "wide"),
    )
    return jax.shard_map(
        on_device,
        mesh=mesh,
        in_specs=placed,
        out_specs=(P("wide", None, "narrow"), P()),
        check_vma=False,
    )
```

time: 579 us -> 246 us (0.42); the launches traced: 572 us -> 245 us
  waiting for transfers between devices: 317 us -> 0 us
  Pallas kernels: 0 us -> 196 us
  other arithmetic: 118 us -> 6.08 us
  matrix products: 36 us -> 0 us
  blocking collectives: 20.5 us -> 0 us
  local copies, waits for them, and re-layouts: 62.7 us -> 42.5 us
  between operations: 16.8 us -> 0.85 us
    psum x2 -> x0, waiting for transfers between devices: 226 us -> none  [the longest x1 185 us: on_device(): gram = lax.psum(gram_term, 'wide')]
    pallas_call x0 -> x4, Pallas kernels: none -> 196 us  [the longest x1 71.4 us: gathers(): pl.pallas_call(gather_kernel, out_shape=[jax.ShapeDtypeStruct((2, 32 * SL...]
    another operation x20 -> x1, other arithmetic: 115 us -> 0.01 us  [the longest x14 73 us: on_device(): lower = jnp.linalg.cholesky(gram)]
    all_gather x2 -> x0, waiting for transfers between devices: 89.8 us -> none  [the longest x1 64 us: on_device(): piece = lax.all_gather(right_edge, 'wide', axis=0, tiled=True)]
    dot_general x6 -> x0, matrix products: 30.1 us -> none  [the longest x1 7.91 us: on_device(): enlarged = jnp.einsum('ivmsdrj,svmew->iderwj', ket_layer, layer)]
    all_gather x2 -> x0, local copies, waits for them, and re-layouts: 23.3 us -> none  [the longest x1 11.7 us: on_device(): piece = lax.all_gather(right_edge, 'wide', axis=0, tiled=True)]
    psum x1 -> x0, blocking collectives: 20.5 us -> none  [on_device(): half_left = lax.psum(partial_value, 'narrow').astype(jnp.bfloat16)]
    another operation x15 -> x0, local copies, waits for them, and re-layouts: 9 us -> none
  transfers between devices with their start and end apart: 4 -> 0, of which waited for: 4 -> 0; matrix products, arithmetic and copies ran while one was open for 11% -> 0% of each run, Pallas kernels for 0% -> 0%
where the time goes in v1:
time: 246 us; the launch traced here: 245 us
  Pallas kernels  196 us (80%)
  local copies, waits for them, and re-layouts  42.5 us (17%)
  other arithmetic  6.08 us (2%)
    pallas_call x1, Pallas kernels, gathers(): pl.pallas_call(gather_kernel, out_shape=[jax.ShapeDtypeStruct((2, 32 * SL...  71.4 us
    pallas_call x1, Pallas kernels, factor(): pl.pallas_call(factor_kernel, out_shape=[jax.ShapeDtypeStruct((448, 448),...  45.2 us
    pallas_call x1, Pallas kernels, sums(): pl.pallas_call(sums_kernel, out_shape=[jax.ShapeDtypeStruct((4, ROWS, 128...  43.8 us
    pallas_call x1, Pallas kernels, contract(): pl.pallas_call(contract_kernel, out_shape=jax.ShapeDtypeStruct((4, ROWS,...  35.5 us
    reshape x1, local copies, waits for them, and re-layouts, layers(): ket.reshape(49, 14, 49, 7)  10.7 us
    unnamed x8, local copies, waits for them, and re-layouts  10.6 us
    reshape x2, local copies, waits for them, and re-layouts, layers(): jnp.pad(ket.reshape(49, 14, 49, 7), ((0, 0), (0, 2), (0, 1), (0, 1)))  7.32 us
    pad x1, local copies, waits for them, and re-layouts, layers(): jnp.pad(ket.reshape(49, 14, 49, 7), ((0, 0), (0, 2), (0, 1), (0, 1)))  6.42 us

profile of v1, /device:TPU:1, one launch (start us, length us, event | category | flops | bytes accessed | tf_op | source)
XLA Modules:
  0.0 245.2 jit_solution(10715229632899175866)
XLA Ops:
  0.7 0.9 reshape.48
  1.8 0.9 pad.41
  2.7 0.1 reshape.46
  2.8 0.9 pad.44
  3.7 1.0 copy.19
  4.9 0.1 copy.20.corner
  5.0 0.9 reshape.52
  5.9 0.7 copy.23
  6.7 0.3 reshape.55
  7.0 0.7 reshape.56.bra
  7.7 0.9 copy.21
  8.7 0.1 pad_select_fusion
  8.8 1.3 fusion.3.pick
  10.1 4.6 %multiply_bitcast_fusion = bf16[7,7,2,7,7,7,7]{5,4,6,3,2,1,0:T(8,128)(2,1)} fusion(bf16[2,7,7,7,7]{2,1,0,4,3:T(8,128)(2,1)S(1)} %copy.21, bf16[7,7]{1,0:T(8,128)(2,1)S(1)} %fusion.4), kind=kLoop, calls=%fused_computation | loop fusion | flops 235298 | bytes 480298 | tf_op jit(solution)/shard_map/suldr,mn->drsmlnu/transpose | solution.py:493
  14.7 10.7 %reshape.53 = bf16[49,14,49,7]{2,3,1,0:T(8,128)(2,1)S(1)} reshape(bf16[7,7,2,7,7,7,7]{5,4,6,3,2,1,0:T(8,128)(2,1)} %multiply_bitcast_fusion) | data formatting | bytes 941192 | tf_op jit(solution)/shard_map/reshape | solution.py:494
  25.4 7.0 %copy.25 = bf16[49,14,49,7]{1,0,3,2:T(8,128)(2,1)} copy(bf16[49,14,49,7]{2,3,1,0:T(8,128)(2,1)S(1)} %reshape.53) | data formatting | bytes 941192
  32.4 6.4 %pad.50.clone = bf16[49,16,50,8]{1,0,3,2:T(8,128)(2,1)} pad(bf16[49,14,49,7]{1,0,3,2:T(8,128)(2,1)} %copy.25, bf16[]{:T(256)} %constant.76.clone.1), padding=0_0x0_2x0_1x0_1 | pad | bytes 1097798 | tf_op jit(solution)/shard_map/jit(_pad)/pad | solution.py:494
  38.8 6.1 %reshape.54 = bf16[784,400]{0,1:T(8,128)(2,1)S(1)} reshape(bf16[49,16,50,8]{1,0,3,2:T(8,128)(2,1)} %pad.50.clone) | data formatting | bytes 1254400 | tf_op jit(solution)/shard_map/reshape | solution.py:494
  44.9 1.2 copy.24.ket
  46.1 71.4 %gathers.1 = (bf16[2,512,3200]{2,1,0:T(8,128)(2,1)}, bf16[2,512,3200]{2,1,0:T(8,128)(2,1)}, bf16[4,400,128]{2,1,0:T(8,128)(2,1)S(1)}, bf16[4,128,512]{2,1,0:T(8,128)(2,1)S(1)}) custom-call(bf16[2,16,3200]{2,1,0:T(8,128)(2,1)S(1)} %get-tuple-element.19.right, bf16[2,16,3200]{2,1,0:T(8,128)(2,1)S(1)} %get-tuple-element.18.warm, ...), custom_call_target="tpu_custom_call" | custom-call | tf_op jit(solution)/shard_map/gathers/pallas_call | solution.py:218
  117.5 0.0 copy-start.1
  117.5 0.8 copy-done.1
  118.3 0.0 copy-start.2
  118.3 0.8 copy-done.2
  119.1 35.5 %contract.1.part = bf16[4,400,128]{2,1,0:T(8,128)(2,1)} custom-call(bf16[2,512,3200]{2,1,0:T(8,128)(2,1)} %get-tuple-element.10.right, bf16[2,512,3200]{2,1,0:T(8,128)(2,1)} %get-tuple-element.11.warm, bf16[4,400,128]{2,1,0:T(8,128)(2,1)} %copy-done.2, bf16[4,128,512]{2,1,0:T(8,128)(2,1)} %copy-done.1, bf16[784,400]{1,0:T(8,128)(2,1)} %copy.24.ket, ...), custom_call_target="tpu_custom_call" | custom-call | tf_op jit(solution)/shard_map/contract/pallas_call | solution.py:294
  154.5 0.0 copy-start
  154.5 1.0 copy-done
  155.5 43.8 %sums.1 = (bf16[4,400,128]{2,1,0:T(8,128)(2,1)S(1)}, f32[4,4,2,64,128]{4,3,2,1,0:T(8,128)S(1)}) custom-call(bf16[4,400,128]{2,1,0:T(8,128)(2,1)S(1)} %copy-done), custom_call_target="tpu_custom_call" | custom-call | tf_op jit(solution)/shard_map/sums/pallas_call | solution.py:390
  199.3 45.2 %factor.1 = (f32[448,448]{1,0:T(8,128)}, f32[400,112]{1,0:T(8,128)S(1)}) custom-call(f32[4,512,128]{2,1,0:T(8,128)S(1)} %bitcast.24, bf16[4,400,128]{2,1,0:T(8,128)(2,1)S(1)} %get-tuple-element.15.proj), custom_call_target="tpu_custom_call" | custom-call | tf_op jit(solution)/shard_map/factor/pallas_call | solution.py:474
  244.5 0.7 reshape.59
  (15 shorter events, 0.2 us)
Async XLA Ops:
  117.5 0.8 copy-start.1
  118.3 0.8 copy-start.2
  154.5 1.0 copy-start

commit v2 on v1

--- a/solution.py
+++ b/solution.py
@@ -37,7 +37,8 @@
     pl.semaphore_wait(barrier, len(peers))
 
 
-def gather_kernel(right, warm, left, corner, right_all, warm_all, left_all, corner_all,
+def gather_kernel(right, warm, left, corner, layer, out,
+                  right_all, warm_all, left_all, corner_all, half, strip, layered, total, ket, bra,
                   paired, merged, pair_s, pair_r, own_s, ring_r, near_s, far_s, yl_s, ys_s, first_s,
                   part_s, part_r, x_s, x_r):
     y, z, core, x = place()
@@ -172,109 +173,139 @@
         arrived(g, 1, ymove(2), zz)
         forward_partner(g, 1, ymove(2), zz)
 
-    def ring(g):
-        y_pass(g, z)
-        for s in (1, 2, 3, 4):
+    def ring_steps(g):
+        steps = [lambda: y_pass(g, z)]
+        for k in (1, 2, 3, 4):
             for way in (1, -1):
-                if way < 0 and s == 4:
+                if way < 0 and k == 4:
                     continue
-                b_ring(g, s, way)
-                for d in range(4):
-                    a_ring(g, s, way, d)
-            if s > 1:
-                y_pass(g, zmove(-(s - 1)))
-                y_pass(g, zmove(s - 1))
-
-    def finish(g):
-        y_pass(g, zmove(-4))
-        for k in range(8):
-            y_last(g, zmove(k))
-
-    for g in (0, 1):
-        begin(g)
-    for g in (0, 1):
-        column(g)
-    for g in (0, 1):
-        ring(g)
-    for g in (0, 1):
-        finish(g)
-    for g in (0, 1):
+                steps.append(functools.partial(b_ring, g, k, way))
+                steps.extend(functools.partial(a_ring, g, k, way, d) for d in range(4))
+            if k > 1:
+                steps.append(functools.partial(y_pass, g, zmove(-(k - 1))))
+                steps.append(functools.partial(y_pass, g, zmove(k - 1)))
+        steps.append(lambda: y_pass(g, zmove(-4)))
+        steps.extend(functools.partial(y_last, g, zmove(k)) for k in range(8))
+        return steps
+
+    def from_partner(g):
         for part in (0, 1):
-            for s in range(32):
-                v = view(g, 1 - core, part, s // 8, s % 8)
-                pltpu.make_async_copy(v, v, part_r.at[g, part, s]).wait()
+            for k in range(32):
+                v = view(g, 1 - core, part, k // 8, k % 8)
+                pltpu.make_async_copy(v, v, part_r.at[g, part, k]).wait()
+
+    begin(0)
+    weights(layer, ket, bra)
+    column(0)
+    steps = ring_steps(0)
+    for step in steps[:-17]:
+        step()
+    begin(1)
+    for step in steps[-17:]:
+        step()
+    column(1)
+    for c in xcopies + own_x:
+        c.wait()
+    acc = jnp.zeros((ROWS, 512), jnp.float32)
+    for n in range(4):
+        acc += jnp.dot(left_all[n], corner_all[n], preferred_element_type=jnp.float32)
+    half[...] = acc.astype(jnp.bfloat16)
+    own_copies[0].wait()
+    from_partner(0)
+
+    work = compute_steps(half, right_all, ket, bra, strip, layered)
+    steps = ring_steps(1)
+    done = 0
+    for k, compute in enumerate(work):
+        compute()
+        upto = len(steps) * (k + 1) // len(work)
+        for step in steps[done:upto]:
+            step()
+        done = upto
+    own_copies[1].wait()
+    from_partner(1)
+    project(strip, warm_all, total, out)
     for c in pending:
         c.wait_send()
-    for c in xcopies:
-        c.wait()
-    for c in own_copies + own_x:
-        c.wait()
-
-
-def gathers(right, warm, left, corner):
-    dma = pltpu.SemaphoreType.DMA
-    any_ = pl.BlockSpec(memory_space=pl.ANY)
-    vm = pl.BlockSpec(memory_space=pltpu.VMEM)
-    return pl.pallas_call(
-        gather_kernel,
-        out_shape=[
-            jax.ShapeDtypeStruct((2, 32 * SLOT, HALF), jnp.bfloat16),
-            jax.ShapeDtypeStruct((2, 32 * SLOT, HALF), jnp.bfloat16),
-            jax.ShapeDtypeStruct((4, ROWS, 128), jnp.bfloat16),
-            jax.ShapeDtypeStruct((4, 128, 512), jnp.bfloat16),
-        ],
-        in_specs=[vm] * 4,
-        out_specs=[any_] * 4,
-        scratch_shapes=[
-            pltpu.VMEM((2, SLOT, HALF), jnp.bfloat16),
-            pltpu.VMEM((2, SLOT, HALF), jnp.bfloat16),
-            dma((2,)), dma((2,)), dma((4,)), dma((2, 2, 32)), dma((2, 2, 32)), dma((2, 2, 32)),
-            dma((2, 2, 32)), dma((2, 2, 32)), dma((2, 3)), dma((2, 2, 32)), dma((2, 2, 32)), dma((2, 3)), dma((2, 3)),
-        ],
-        compiler_params=pltpu.CompilerParams(collective_id=1, has_side_effects=True, vmem_limit_bytes=48 * MIB),
-        name="gathers",
-    )(right, warm, left, corner)
-
-
-def contract_kernel(right, warm, left, corner, ket, bra, pick, out, half, strip, layered, enlarged, total):
-    acc = jnp.zeros((ROWS, 512), jnp.float32)
-    for n in range(4):
-        acc += jnp.dot(left[n], corner[n], preferred_element_type=jnp.float32)
-    half[...] = acc.astype(jnp.bfloat16)
-
-    for h in range(2):
-        @pl.loop(0, 5)
-        def _(chunk):
-            cols = pl.ds(pl.multiple_of(chunk * 640, 640), 640)
-            res = jnp.dot(half[...], right[h, :, cols], preferred_element_type=jnp.float32)
-            for j in range(5):
-                rows = pl.ds(pl.multiple_of((h * 25 + chunk * 5 + j) * 8, 8), 8)
-                strip[:, rows, :] = res[:, j * 128:(j + 1) * 128].reshape(50, 8, 128)
-
-    @pl.loop(0, 25)
-    def _(t):
-        x = jnp.concatenate([strip[2 * t].astype(jnp.bfloat16), strip[2 * t + 1].astype(jnp.bfloat16)], axis=1)
-        res = jnp.dot(ket[...], x, preferred_element_type=jnp.float32).astype(jnp.bfloat16)
-        for j in range(2):
-            rows = pl.ds(pl.multiple_of((2 * t + j) * 16, 16), 16)
-            layered[:, rows, :] = res[:, j * 128:(j + 1) * 128].reshape(49, 16, 128)
-
-    enlarged[49] = jnp.zeros((ROWS, 128), jnp.float32)
-
-    @pl.loop(0, 50)
-    def _(b):
-        enlarged[b, 392:400, :] = jnp.zeros((8, 128), jnp.float32)
-
-    @pl.loop(0, 49)
-    def _(dr):
-        d, r = lax.div(dr, 7), lax.rem(dr, 7)
-        x = jnp.concatenate([layered[dr, i * 112:(i + 1) * 112, :] for i in range(7)], axis=1)
-        res = jnp.dot(bra[...], x, preferred_element_type=jnp.float32)
-        for i in range(7):
-            rows = pl.ds(pl.multiple_of((i * 7 + d) * 8, 8), 8)
-            for s in range(7):
-                enlarged[r * 7 + s, rows, :] = res[s * 8:(s + 1) * 8, i * 128:(i + 1) * 128]
-
+
+
+def iota(shape, axis):
+    return lax.broadcasted_iota(jnp.int32, shape, axis)
+
+
+def flags(mask):
+    return jnp.where(mask, 1.0, 0.0).astype(jnp.bfloat16)
+
+
+def mm(a, b):
+    return jnp.dot(a, b, preferred_element_type=jnp.float32).astype(jnp.bfloat16)
+
+
+def mm_nt(a, b):
+    return lax.dot_general(a, b, (((1,), (1,)), ((), ())), preferred_element_type=jnp.float32).astype(jnp.bfloat16)
+
+
+def weights(layer, ket, bra):
+    row, col = iota((784, 49), 0), iota((784, 49), 1)
+    low = row & 15
+    spread = mm_nt(flags((row >> 4 == col) & (low < 7)), layer[0])
+    spread += mm_nt(flags((row >> 4 == col) & (low >= 7) & (low < 14)), layer[1])
+    row, col = iota((49, ROWS), 0), iota((49, ROWS), 1)
+    q, u = col >> 3, col & 7
+    full = mm(spread, flags((u < 7) & (q < 49) & (row == u * 7 + ((q * 37) >> 8))))
+    row, col = iota((784, ROWS), 0), iota((784, ROWS), 1)
+    low, q = row & 15, col >> 3
+    same = jnp.where(low < 7, low, low - 7) == q - 7 * ((q * 37) >> 8)
+    ket[...] = jnp.where(same, full.astype(jnp.float32), 0.0).astype(jnp.bfloat16)
+    row, col = iota((56, 49), 0), iota((56, 49), 1)
+    lead = flags((row & 7 < 7) & (col == (row & 7) * 7 + (row >> 3)))
+    row, col = iota((49, 112), 0), iota((49, 112), 1)
+    low = col & 15
+    acc = jnp.zeros((56, 112), jnp.float32)
+    for s in range(2):
+        ok = (low >= 7 * s) & (low < 7 * s + 7) & (row == (col >> 4) * 7 + low - 7 * s)
+        acc += mm(mm_nt(lead, layer[s]), flags(ok)).astype(jnp.float32)
+    bra[...] = acc.astype(jnp.bfloat16)
+
+
+def compute_steps(half, right, ket, bra, strip, layered):
+    def strips(h, chunk):
+        res = jnp.dot(half[...], right[h, :, chunk * 640:(chunk + 1) * 640], preferred_element_type=jnp.float32)
+        for j in range(5):
+            first = (h * 25 + chunk * 5 + j) * 8
+            strip[:, first:first + 8, :] = res[:, j * 128:(j + 1) * 128].reshape(50, 8, 128)
+
+    def kets(first):
+        @pl.loop(first, first + 5)
+        def _(t):
+            x = jnp.concatenate([strip[2 * t].astype(jnp.bfloat16), strip[2 * t + 1].astype(jnp.bfloat16)], axis=1)
+            res = jnp.dot(ket[...], x, preferred_element_type=jnp.float32).astype(jnp.bfloat16)
+            for j in range(2):
+                rows = pl.ds(pl.multiple_of((2 * t + j) * 16, 16), 16)
+                layered[:, rows, :] = res[:, j * 128:(j + 1) * 128].reshape(49, 16, 128)
+
+    def clear():
+        strip[49] = jnp.zeros((ROWS, 128), jnp.float32)
+        strip[:, 392:400, :] = jnp.zeros((50, 8, 128), jnp.float32)
+
+    def bras(d):
+        @pl.loop(0, 7)
+        def _(r):
+            x = jnp.concatenate([layered[d * 7 + r, i * 112:(i + 1) * 112, :] for i in range(7)], axis=1)
+            res = jnp.dot(bra[...], x, preferred_element_type=jnp.float32)
+            for i in range(7):
+                for s in range(7):
+                    strip[r * 7 + s, (i * 7 + d) * 8:(i * 7 + d) * 8 + 8, :] = (
+                        res[s * 8:(s + 1) * 8, i * 128:(i + 1) * 128])
+
+    work = [functools.partial(strips, h, chunk) for h in range(2) for chunk in range(5)]
+    work += [functools.partial(kets, 5 * t) for t in range(5)]
+    work += [clear]
+    work += [functools.partial(bras, d) for d in range(7)]
+    return work
+
+
+def project(enlarged, warm, total, out):
     total[...] = jnp.zeros_like(total)
     for h in range(2):
         @pl.loop(0, 5)
@@ -284,28 +315,41 @@
                 [enlarged[h * 25 + chunk * 5 + j].astype(jnp.bfloat16) for j in range(5)], axis=1)
             total[...] += lax.dot_general(x, warm[h, :, cols], (((1,), (1,)), ((), ())),
                                           preferred_element_type=jnp.float32)
-    res = jnp.dot(total[...].astype(jnp.bfloat16), pick[...], preferred_element_type=jnp.float32)
+    row, col = iota((512, 512), 0), iota((512, 512), 1)
+    held = jnp.where(row & 15 < 14, (row >> 4) * 14 + (row & 15), -1)
+    pick = flags(held == jnp.where(col & 127 < 112, (col >> 7) * 112 + (col & 127), -2))
+    res = mm(total[...].astype(jnp.bfloat16), pick)
     for n in range(4):
-        out[n] = res[:, n * 128:(n + 1) * 128].astype(jnp.bfloat16)
-
-
-def contract(right, warm, left, corner, ket, bra, pick):
+        out[n] = res[:, n * 128:(n + 1) * 128]
+
+
+def gathers(right, warm, left, corner, layer):
+    dma = pltpu.SemaphoreType.DMA
     vm = pl.BlockSpec(memory_space=pltpu.VMEM)
     return pl.pallas_call(
-        contract_kernel,
+        gather_kernel,
         out_shape=jax.ShapeDtypeStruct((4, ROWS, 128), jnp.bfloat16),
-        in_specs=[vm] * 7,
+        in_specs=[vm] * 5,
         out_specs=vm,
         scratch_shapes=[
+            pltpu.VMEM((2, 32 * SLOT, HALF), jnp.bfloat16),
+            pltpu.VMEM((2, 32 * SLOT, HALF), jnp.bfloat16),
+            pltpu.VMEM((4, ROWS, 128), jnp.bfloat16),
+            pltpu.VMEM((4, 128, 512), jnp.bfloat16),
             pltpu.VMEM((ROWS, 512), jnp.bfloat16),
             pltpu.VMEM((50, ROWS, 128), jnp.float32),
             pltpu.VMEM((49, 800, 128), jnp.bfloat16),
-            pltpu.VMEM((50, ROWS, 128), jnp.float32),
             pltpu.VMEM((ROWS, 512), jnp.float32),
+            pltpu.VMEM((784, ROWS), jnp.bfloat16),
+            pltpu.VMEM((56, 112), jnp.bfloat16),
+            pltpu.VMEM((2, SLOT, HALF), jnp.bfloat16),
+            pltpu.VMEM((2, SLOT, HALF), jnp.bfloat16),
+            dma((2,)), dma((2,)), dma((4,)), dma((2, 2, 32)), dma((2, 2, 32)), dma((2, 2, 32)),
+            dma((2, 2, 32)), dma((2, 2, 32)), dma((2, 3)), dma((2, 2, 32)), dma((2, 2, 32)), dma((2, 3)), dma((2, 3)),
         ],
-        compiler_params=pltpu.CompilerParams(vmem_limit_bytes=60 * MIB),
-        name="contract",
-    )(right, warm, left, corner, ket, bra, pick)
+        compiler_params=pltpu.CompilerParams(collective_id=1, has_side_effects=True, vmem_limit_bytes=58 * MIB),
+        name="gathers",
+    )(right, warm, left, corner, layer)
 
 
 def sums_kernel(part, proj, gram, got, slab, got1, piece, got2, n_s, n_r, p_s, p_r, a_s, a_r, b_s, b_r,
@@ -487,24 +531,6 @@
     return jnp.where(core == 0, jnp.pad(rows, ((0, 0), (0, 9), (0, 0))), jnp.pad(rows, ((0, 0), (7, 2), (0, 0))))
 
 
-def layers(single_layer):
-    layer = single_layer.reshape(2, BOND, BOND, BOND, BOND)
-    eye = jnp.eye(BOND, dtype=layer.dtype)
-    ket = jnp.einsum("suldr,mn->drsmlnu", layer, eye)
-    ket = jnp.pad(ket.reshape(49, 14, 49, 7), ((0, 0), (0, 2), (0, 1), (0, 1))).reshape(784, ROWS)
-    bra = layer.transpose(4, 3, 1, 0, 2).reshape(7, 7, 7, 14)
-    bra = jnp.pad(bra, ((0, 0), (0, 1), (0, 0), (0, 2))).reshape(56, 112)
-    return ket, bra
-
-
-def picker():
-    at = lax.broadcasted_iota(jnp.int32, (512, 512), 0)
-    to = lax.broadcasted_iota(jnp.int32, (512, 512), 1)
-    held = jnp.where(at % 16 < 14, at // 16 * 14 + at % 16, -1)
-    wanted = jnp.where(to % 128 < 112, to // 128 * 112 + to % 128, -2)
-    return (held == wanted).astype(jnp.bfloat16)
-
-
 def on_device(left_edge, corner, right_edge, single_layer, warm_basis):
     core = lax.axis_index("wide") % 2
     right = shard_rows(right_edge, core)
@@ -513,9 +539,7 @@
     left = jnp.pad(left, ((0, 0), (0, 0), (0, 1), (0, 16))).reshape(392, 128)
     left = jnp.pad(left, ((0, 8), (0, 0)))
     corner = jnp.pad(corner.reshape(112, 32, 14), ((0, 16), (0, 0), (0, 2))).reshape(128, 512)
-    ket, bra = layers(single_layer)
-    right, warm, left, corner = gathers(right, warm, left, corner)
-    part = contract(right, warm, left, corner, ket, bra, picker())
+    part = gathers(right, warm, left, corner, single_layer.reshape(2, 49, 49))
     proj, gram = sums(part)
     r_factor, rows = factor(gram.reshape(4, 512, 128), proj)
     new_basis = rows[:392].reshape(7, 7, 8, 112)[:, :, :7].reshape(7, 49, 112)

time: 246 us -> 187 us (0.76)
  local copies, waits for them, and re-layouts: 42.5 us -> 7.09 us
  Pallas kernels: 196 us -> 178 us
  other arithmetic: 6.08 us -> 0.88 us
    reshape x7 -> x1, local copies, waits for them, and re-layouts: 20.8 us -> 0.75 us  [on_device(): part = gathers(right, warm, left, corner, single_layer.reshape(2, 49, 49))]
    pallas_call x2 -> x1, Pallas kernels: 107 us -> 89.6 us  [gathers(): pl.pallas_call(gather_kernel, out_shape=jax.ShapeDtypeStruct((4, ROWS, 12...]
    unnamed x8 -> x11, local copies, waits for them, and re-layouts: 10.6 us -> 2.96 us
    pad x2 -> x0, local copies, waits for them, and re-layouts: 6.45 us -> none  [the longest x1 6.42 us: layers(): jnp.pad(ket.reshape(49, 14, 49, 7), ((0, 0), (0, 2), (0, 1), (0, 1)))]
    transpose x1 -> x0, other arithmetic: 4.58 us -> none  [layers(): ket = jnp.einsum('suldr,mn->drsmlnu', layer, eye)]
where the time goes in v2:
time: 187 us
  Pallas kernels  178 us (95%)
  local copies, waits for them, and re-layouts  7.09 us (4%)
    pallas_call x1, Pallas kernels, gathers(): pl.pallas_call(gather_kernel, out_shape=jax.ShapeDtypeStruct((4, ROWS, 12...  89.6 us
    pallas_call x1, Pallas kernels, factor(): pl.pallas_call(factor_kernel, out_shape=[jax.ShapeDtypeStruct((448, 448),...  45.4 us
    pallas_call x1, Pallas kernels, sums(): pl.pallas_call(sums_kernel, out_shape=[jax.ShapeDtypeStruct((4, ROWS, 128...  43.3 us

profile of v2, /device:TPU:1, one launch (start us, length us, event | category | flops | bytes accessed | tf_op | source)
XLA Modules:
  0.0 187.0 jit_solution(5672396322681281749)
XLA Ops:
  0.6 0.0 copy-start.4
  0.7 0.7 copy-done.4
  1.3 0.7 reshape.40.layer
  2.1 0.9 reshape.36
  3.1 0.0 copy-start.2
  3.1 0.6 pad.40.left
  3.8 0.3 copy-done.2
  4.0 0.1 reshape.34
  4.2 0.0 copy-start.3
  4.2 0.0 copy-start.1
  4.2 0.9 copy-done.3
  5.1 0.0 copy-done.1
  5.1 0.1 copy.10
  5.3 0.8 copy.11.corner
  6.1 0.9 pad_select_fusion
  7.0 89.6 %gathers.1.part = bf16[4,400,128]{2,1,0:T(8,128)(2,1)} custom-call(bf16[2,16,3200]{2,1,0:T(8,128)(2,1)} %get-tuple-element.11.right, bf16[2,16,3200]{2,1,0:T(8,128)(2,1)} %get-tuple-element.10.warm, bf16[400,128]{1,0:T(8,128)(2,1)} %pad.40.left, bf16[128,512]{1,0:T(8,128)(2,1)} %copy.11.corner, bf16[2,49,49]{2,1,0:T(8,128)(2,1)} %reshape.40.layer), custom_call_target="tpu_custom_call" | custom-call | tf_op jit(solution)/shard_map/gathers/pallas_call | solution.py:329
  96.6 0.0 copy-start
  96.6 1.0 copy-done
  97.6 43.3 %sums.1 = (bf16[4,400,128]{2,1,0:T(8,128)(2,1)S(1)}, f32[4,4,2,64,128]{4,3,2,1,0:T(8,128)S(1)}) custom-call(bf16[4,400,128]{2,1,0:T(8,128)(2,1)S(1)} %copy-done), custom_call_target="tpu_custom_call" | custom-call | tf_op jit(solution)/shard_map/sums/pallas_call | solution.py:434
  140.9 45.4 %factor.1 = (f32[448,448]{1,0:T(8,128)}, f32[400,112]{1,0:T(8,128)S(1)}) custom-call(f32[4,512,128]{2,1,0:T(8,128)S(1)} %bitcast.17, bf16[4,400,128]{2,1,0:T(8,128)(2,1)S(1)} %get-tuple-element.7.proj), custom_call_target="tpu_custom_call" | custom-call | tf_op jit(solution)/shard_map/factor/pallas_call | solution.py:518
  186.3 0.7 reshape.43
  (8 shorter events, 0.2 us)
Async XLA Ops:
  0.6 0.7 copy-start.4
  3.1 0.9 copy-start.2
  4.2 0.9 copy-start.3
  4.2 0.9 copy-start.1
  96.6 1.0 copy-start

commit v3 on v2

--- a/solution.py
+++ b/solution.py
@@ -37,10 +37,11 @@
     pl.semaphore_wait(barrier, len(peers))
 
 
-def gather_kernel(right, warm, left, corner, layer, out,
+def gather_kernel(right, warm, left, corner, layer, proj, gram,
                   right_all, warm_all, left_all, corner_all, half, strip, layered, total, ket, bra,
-                  paired, merged, pair_s, pair_r, own_s, ring_r, near_s, far_s, yl_s, ys_s, first_s,
-                  part_s, part_r, x_s, x_r):
+                  paired, merged, part, got, slab, got1, piece, got2,
+                  pair_s, pair_r, own_s, ring_r, ring_s, part_s, part_r, x_s, x_r,
+                  n_s, n_r, p_s, p_r, a_s, a_r, b_s, b_r, c_s, c_r, d_s, d_r, f_s, f_r):
     y, z, core, x = place()
     zdir = 1 - 2 * core
 
@@ -54,17 +55,18 @@
         return (wide_of(yy, zz, core if cc is None else cc), x)
 
     partner = at(y, z, 1 - core)
-    peers = [partner, at(y, zmove(1)), at(y, zmove(-1)), at(ymove(1), z), at(ymove(2), z), at(ymove(3), z)]
-    peers += [(wide_of(y, z, core), lax.rem(x + d, 4)) for d in (1, 2, 3)]
-    greet(peers)
-
-    pending = []
+    others = [(lax.rem(y + k // 2, 4), lax.rem(core + k % 2, 2)) for k in range(1, 8)]
+    xs = [lax.rem(x + d, 4) for d in (1, 2, 3)]
+    zs = [lax.rem(z + d, 8) for d in range(1, 8)]
+    me = wide_of(y, z, core)
+    plane = [(lax.rem(x + k // 4, 4), lax.rem(y + k % 4, 4)) for k in (10, 2, 8, 6, 14, 9, 11, 1, 3, 4, 12, 5, 7, 13, 15)]
+    greet([at(yy, z, cc) for yy, cc in others] + [at(y, zz) for zz in zs]
+          + [(wide_of(lax.rem(y + k % 4, 4), z, core), lax.rem(x + k // 4, 4)) for k in range(4, 16)])
 
     def push(src, dst, ss, rs, device):
         c = pltpu.make_async_remote_copy(src_ref=src, dst_ref=dst, send_sem=ss, recv_sem=rs,
                                          device_id=device, device_id_type=MESH)
         c.start()
-        pending.append(c)
 
     arrays = ((right, right_all), (warm, warm_all))
     pairs = []
@@ -97,13 +99,13 @@
     def slot(yy, zz):
         return yy * 8 + zz
 
-    def send(g, part, yy, zz, sem, device, src=None):
+    def send(g, part, yy, zz, device, src=None):
         v = view(g, core, part, yy, zz)
-        push(v if src is None else src, v, sem.at[g, part, slot(yy, zz)], ring_r.at[g, part, slot(yy, zz)], device)
+        push(v if src is None else src, v, ring_s.at[g], ring_r.at[g, part, slot(yy, zz)], device)
 
     def forward_partner(g, part, yy, zz, src=None):
         v = view(g, core, part, yy, zz)
-        push(v if src is None else src, v, part_s.at[g, part, slot(yy, zz)], part_r.at[g, part, slot(yy, zz)], partner)
+        push(v if src is None else src, v, part_s.at[g], part_r.at[g], partner)
 
     def arrived(g, part, yy, zz):
         v = view(g, core, part, yy, zz)
@@ -123,13 +125,13 @@
         a, b = merged.at[g, :, 0:A_LANES], merged.at[g, :, A_LANES:HALF]
         va = view(g, core, 0, y, z)
         for d in (1, 2, 3):
-            push(a, va, first_s.at[g, d - 1], ring_r.at[g, 0, slot(y, z)], at(ymove(d), z))
-        send(g, 1, y, z, near_s, znext, b)
-        send(g, 1, y, z, far_s, zprev, b)
-        send(g, 0, y, z, near_s, znext, a)
-        send(g, 0, y, z, far_s, zprev, a)
-        send(g, 1, y, z, yl_s, ynext, b)
-        send(g, 1, y, z, ys_s, yprev, b)
+            push(a, va, ring_s.at[g], ring_r.at[g, 0, slot(y, z)], at(ymove(d), z))
+        send(g, 1, y, z, znext, b)
+        send(g, 1, y, z, zprev, b)
+        send(g, 0, y, z, znext, a)
+        send(g, 0, y, z, zprev, a)
+        send(g, 1, y, z, ynext, b)
+        send(g, 1, y, z, yprev, b)
         forward_partner(g, 0, y, z, a)
         forward_partner(g, 1, y, z, b)
 
@@ -137,19 +139,19 @@
         for d in (1, 2, 3):
             yy = ymove(d)
             arrived(g, 0, yy, z)
-            send(g, 0, yy, z, near_s, znext)
-            send(g, 0, yy, z, far_s, zprev)
+            send(g, 0, yy, z, znext)
+            send(g, 0, yy, z, zprev)
             forward_partner(g, 0, yy, z)
 
     def b_ring(g, s, way):
         zz = zmove(-s) if way > 0 else zmove(s)
         arrived(g, 1, y, zz)
         if way > 0 and s < 4:
-            send(g, 1, y, zz, near_s, znext)
+            send(g, 1, y, zz, znext)
         if way < 0 and s < 3:
-            send(g, 1, y, zz, far_s, zprev)
-        send(g, 1, y, zz, yl_s, ynext)
-        send(g, 1, y, zz, ys_s, yprev)
+            send(g, 1, y, zz, zprev)
+        send(g, 1, y, zz, ynext)
+        send(g, 1, y, zz, yprev)
         forward_partner(g, 1, y, zz)
 
     def a_ring(g, s, way, d):
@@ -157,14 +159,14 @@
         yy = ymove(d)
         arrived(g, 0, yy, zz)
         if way > 0 and s < 4:
-            send(g, 0, yy, zz, near_s, znext)
+            send(g, 0, yy, zz, znext)
         if way < 0 and s < 3:
-            send(g, 0, yy, zz, far_s, zprev)
+            send(g, 0, yy, zz, zprev)
         forward_partner(g, 0, yy, zz)
 
     def y_pass(g, zz):
         arrived(g, 1, ymove(-1), zz)
-        send(g, 1, ymove(-1), zz, yl_s, ynext)
+        send(g, 1, ymove(-1), zz, ynext)
         forward_partner(g, 1, ymove(-1), zz)
         arrived(g, 1, ymove(1), zz)
         forward_partner(g, 1, ymove(1), zz)
@@ -189,10 +191,10 @@
         return steps
 
     def from_partner(g):
-        for part in (0, 1):
-            for k in range(32):
-                v = view(g, 1 - core, part, k // 8, k % 8)
-                pltpu.make_async_copy(v, v, part_r.at[g, part, k]).wait()
+        settle(arrays[g][1].at[1 - core], part_r.at[g])
+
+    def settle(ref, sem):
+        pltpu.make_async_copy(ref, ref, sem).wait()
 
     begin(0)
     weights(layer, ket, bra)
@@ -224,9 +226,76 @@
         done = upto
     own_copies[1].wait()
     from_partner(1)
-    project(strip, warm_all, total, out)
-    for c in pending:
+
+    def start(src, dst, ss, rs, device):
+        c = pltpu.make_async_remote_copy(src_ref=src, dst_ref=dst, send_sem=ss, recv_sem=rs,
+                                         device_id=device, device_id_type=MESH)
+        c.start()
+        return c
+
+    c1 = [None] * 3
+    for pair in ((1, 0), (2, None)):
+        names = [x if d is None else xs[d] for d in pair]
+        project(strip, warm_all, total, part, names)
+        for d in pair:
+            if d is not None:
+                c1[d] = start(part.at[xs[d]], got.at[d], n_s.at[d], n_r.at[d], (me, xs[d]))
+    acc = part[x].astype(jnp.float32)
+    for d in range(3):
+        c1[d].wait_recv()
+        acc += got[d].astype(jnp.float32)
+    proj[x] = acc.astype(jnp.bfloat16)
+    c2 = [start(proj.at[x], proj.at[x], p_s.at[d], p_r.at[d], (me, xs[d])) for d in range(3)]
+    own = acc.astype(jnp.bfloat16)
+    tn = (((0,), (0,)), ((), ()))
+    scale = 1.0 / (448 * 49)
+
+    def product(n):
+        slab[pl.ds(pl.multiple_of(n * 128, 128), 128), :] = lax.dot_general(
+            proj[n], own, tn, preferred_element_type=jnp.float32) * scale
+
+    product(x)
+    for d in (0, 2, 1):
+        c2[d].wait_recv()
+        product(lax.rem(x + 3 - d, 4))
+
+    def rows(k, size):
+        return pl.ds(pl.multiple_of(k * size, size), size)
+
+    mine = y * 2 + core
+    c3 = [start(slab.at[rows(yy * 2 + cc, 64)], got1.at[k], a_s.at[k], a_r.at[k], (wide_of(yy, z, cc), x))
+          for k, (yy, cc) in enumerate(others)]
+    acc = slab[rows(mine, 64), :]
+    for k in range(7):
+        c3[k].wait_recv()
+        acc += got1[k]
+    piece[...] = acc
+    c4 = [start(piece.at[rows(zz, 8)], got2.at[k], b_s.at[k], b_r.at[k], (wide_of(y, zz, core), x))
+          for k, zz in enumerate(zs)]
+    acc = piece[rows(z, 8), :]
+    for k in range(7):
+        c4[k].wait_recv()
+        acc += got2[k]
+    spot = gram.at[x, y, core, rows(z, 8)]
+    gram[x, y, core, rows(z, 8), :] = acc
+    c5 = [start(spot, spot, c_s.at[k], c_r.at[k], at(y, zz)) for k, zz in enumerate(zs)]
+    for c in c5:
+        c.wait_recv()
+    spot = gram.at[x, y, core]
+    c6 = [start(spot, spot, d_s.at[k], d_r.at[k], (wide_of(yy, z, core), xx)) for k, (xx, yy) in enumerate(plane)]
+    start(spot, spot, f_s, f_r, partner)
+    for k in (7, 8, 9, 10, 2, 1, 11, 12, 13, 14, 3, 4, 5, 6, 0):
+        xx, yy = plane[k]
+        c6[k].wait_recv()
+        spot = gram.at[lax.rem(2 * x + 4 - xx, 4), lax.rem(2 * y + 4 - yy, 4), core]
+        start(spot, spot, f_s, f_r, partner)
+    settle(gram.at[:, :, core], f_s)
+    settle(gram.at[:, :, 1 - core], f_r)
+    for c in c1 + c2 + c3 + c4 + c5 + c6:
         c.wait_send()
+    for g in (0, 1):
+        settle(arrays[g][1].at[core], part_s.at[g])
+        settle(arrays[g][1].at[core, 0:496], ring_s.at[g])
 
 
 def iota(shape, axis):
@@ -305,22 +374,21 @@
     return work
 
 
-def project(enlarged, warm, total, out):
+def project(enlarged, warm, total, part, names):
     total[...] = jnp.zeros_like(total)
+    spans = [pl.ds(pl.multiple_of(n * 128, 128), 128) for n in names]
     for h in range(2):
         @pl.loop(0, 5)
         def _(chunk):
             cols = pl.ds(pl.multiple_of(chunk * 640, 640), 640)
             x = jnp.concatenate(
                 [enlarged[h * 25 + chunk * 5 + j].astype(jnp.bfloat16) for j in range(5)], axis=1)
-            total[...] += lax.dot_general(x, warm[h, :, cols], (((1,), (1,)), ((), ())),
-                                          preferred_element_type=jnp.float32)
-    row, col = iota((512, 512), 0), iota((512, 512), 1)
-    held = jnp.where(row & 15 < 14, (row >> 4) * 14 + (row & 15), -1)
-    pick = flags(held == jnp.where(col & 127 < 112, (col >> 7) * 112 + (col & 127), -2))
-    res = mm(total[...].astype(jnp.bfloat16), pick)
-    for n in range(4):
-        out[n] = res[:, n * 128:(n + 1) * 128]
+            w = jnp.concatenate([warm[h, span, cols] for span in spans], axis=0)
+            total[...] += lax.dot_general(x, w, (((1,), (1,)), ((), ())), preferred_element_type=jnp.float32)
+    row, col = iota((128, 128), 0), iota((128, 128), 1)
+    pick = flags((row & 15 < 14) & (col == (row >> 4) * 14 + (row & 15)))
+    for k, n in enumerate(names):
+        part[n] = mm(total[:, k * 128:(k + 1) * 128].astype(jnp.bfloat16), pick)
 
 
 def gathers(right, warm, left, corner, layer):
@@ -328,9 +396,12 @@
     vm = pl.BlockSpec(memory_space=pltpu.VMEM)
     return pl.pallas_call(
         gather_kernel,
-        out_shape=jax.ShapeDtypeStruct((4, ROWS, 128), jnp.bfloat16),
+        out_shape=[
+            jax.ShapeDtypeStruct((4, ROWS, 128), jnp.bfloat16),
+            jax.ShapeDtypeStruct((4, 4, 2, 64, 128), jnp.float32),
+        ],
         in_specs=[vm] * 5,
-        out_specs=vm,
+        out_specs=[vm, vm],
         scratch_shapes=[
             pltpu.VMEM((2, 32 * SLOT, HALF), jnp.bfloat16),
             pltpu.VMEM((2, 32 * SLOT, HALF), jnp.bfloat16),
@@ -339,118 +410,24 @@
             pltpu.VMEM((ROWS, 512), jnp.bfloat16),
             pltpu.VMEM((50, ROWS, 128), jnp.float32),
             pltpu.VMEM((49, 800, 128), jnp.bfloat16),
-            pltpu.VMEM((ROWS, 512), jnp.float32),
+            pltpu.VMEM((ROWS, 256), jnp.float32),
             pltpu.VMEM((784, ROWS), jnp.bfloat16),
             pltpu.VMEM((56, 112), jnp.bfloat16),
             pltpu.VMEM((2, SLOT, HALF), jnp.bfloat16),
             pltpu.VMEM((2, SLOT, HALF), jnp.bfloat16),
-            dma((2,)), dma((2,)), dma((4,)), dma((2, 2, 32)), dma((2, 2, 32)), dma((2, 2, 32)),
-            dma((2, 2, 32)), dma((2, 2, 32)), dma((2, 3)), dma((2, 2, 32)), dma((2, 2, 32)), dma((2, 3)), dma((2, 3)),
-        ],
-        compiler_params=pltpu.CompilerParams(collective_id=1, has_side_effects=True, vmem_limit_bytes=58 * MIB),
-        name="gathers",
-    )(right, warm, left, corner, layer)
-
-
-def sums_kernel(part, proj, gram, got, slab, got1, piece, got2, n_s, n_r, p_s, p_r, a_s, a_r, b_s, b_r,
-                c_s, c_r, d_s, d_r, e_s, e_r, f_s, f_r):
-    y, z, core, x = place()
-    others = [(lax.rem(y + k // 2, 4), lax.rem(core + k % 2, 2)) for k in range(1, 8)]
-    xs = [lax.rem(x + d, 4) for d in (1, 2, 3)]
-    zs = [lax.rem(z + d, 8) for d in range(1, 8)]
-    me = wide_of(y, z, core)
-    greet([(me, xx) for xx in xs] + [(wide_of(yy, z, cc), x) for yy, cc in others]
-          + [(wide_of(y, zz, core), x) for zz in zs])
-
-    def start(src, dst, ss, rs, device):
-        c = pltpu.make_async_remote_copy(src_ref=src, dst_ref=dst, send_sem=ss, recv_sem=rs,
-                                         device_id=device, device_id_type=MESH)
-        c.start()
-        return c
-
-    c1 = [start(part.at[xs[d]], got.at[d], n_s.at[d], n_r.at[d], (me, xs[d])) for d in range(3)]
-    acc = part[x].astype(jnp.float32)
-    for d in range(3):
-        c1[d].wait_recv()
-        acc += got[d].astype(jnp.float32)
-    proj[x] = acc.astype(jnp.bfloat16)
-    c2 = [start(proj.at[x], proj.at[x], p_s.at[d], p_r.at[d], (me, xs[d])) for d in range(3)]
-    own = acc.astype(jnp.bfloat16)
-    tn = (((0,), (0,)), ((), ()))
-    scale = 1.0 / (448 * 49)
-
-    def product(n):
-        slab[pl.ds(pl.multiple_of(n * 128, 128), 128), :] = lax.dot_general(
-            proj[n], own, tn, preferred_element_type=jnp.float32) * scale
-
-    product(x)
-    for d in (0, 2, 1):
-        c2[d].wait_recv()
-        product(lax.rem(x + 3 - d, 4))
-
-    def rows(k, size):
-        return pl.ds(pl.multiple_of(k * size, size), size)
-
-    mine = y * 2 + core
-    c3 = [start(slab.at[rows(yy * 2 + cc, 64)], got1.at[k], a_s.at[k], a_r.at[k], (wide_of(yy, z, cc), x))
-          for k, (yy, cc) in enumerate(others)]
-    acc = slab[rows(mine, 64), :]
-    for k in range(7):
-        c3[k].wait_recv()
-        acc += got1[k]
-    piece[...] = acc
-    c4 = [start(piece.at[rows(zz, 8)], got2.at[k], b_s.at[k], b_r.at[k], (wide_of(y, zz, core), x))
-          for k, zz in enumerate(zs)]
-    acc = piece[rows(z, 8), :]
-    for k in range(7):
-        c4[k].wait_recv()
-        acc += got2[k]
-    spot = gram.at[x, y, core, rows(z, 8)]
-    gram[x, y, core, rows(z, 8), :] = acc
-    c5 = [start(spot, spot, c_s.at[k], c_r.at[k], (wide_of(y, zz, core), x)) for k, zz in enumerate(zs)]
-    for c in c5:
-        c.wait_recv()
-    spot = gram.at[x, y, core]
-    c6 = [start(spot, spot, d_s.at[d], d_r.at[d], (me, xs[d])) for d in range(3)]
-    for c in c6:
-        c.wait_recv()
-    spot = gram.at[:, y, core]
-    c7 = [start(spot, spot, e_s.at[d - 1], e_r.at[d - 1], (wide_of(lax.rem(y + d, 4), z, core), x)) for d in (1, 2, 3)]
-    other = (wide_of(y, z, 1 - core), x)
-    c8 = [start(spot, spot, f_s.at[0], f_r.at[0], other)]
-    for d in (3, 1, 2):
-        c7[d - 1].wait_recv()
-        spot = gram.at[:, lax.rem(y + 4 - d, 4), core]
-        c8.append(start(spot, spot, f_s.at[d], f_r.at[d], other))
-    for c in c8:
-        c.wait()
-    for c in c1 + c2 + c3 + c4 + c5 + c6 + c7:
-        c.wait_send()
-
-
-def sums(part):
-    dma = pltpu.SemaphoreType.DMA
-    vm = pl.BlockSpec(memory_space=pltpu.VMEM)
-    return pl.pallas_call(
-        sums_kernel,
-        out_shape=[
-            jax.ShapeDtypeStruct((4, ROWS, 128), jnp.bfloat16),
-            jax.ShapeDtypeStruct((4, 4, 2, 64, 128), jnp.float32),
-        ],
-        in_specs=[vm],
-        out_specs=[vm, vm],
-        scratch_shapes=[
+            pltpu.VMEM((4, ROWS, 128), jnp.bfloat16),
             pltpu.VMEM((3, ROWS, 128), jnp.bfloat16),
             pltpu.VMEM((512, 128), jnp.float32),
             pltpu.VMEM((7, 64, 128), jnp.float32),
             pltpu.VMEM((64, 128), jnp.float32),
             pltpu.VMEM((7, 8, 128), jnp.float32),
+            dma((2,)), dma((2,)), dma((4,)), dma((2, 2, 32)), dma((2,)), dma((2,)), dma((2,)), dma((2, 3)), dma((2, 3)),
             dma((3,)), dma((3,)), dma((3,)), dma((3,)), dma((7,)), dma((7,)), dma((7,)), dma((7,)),
-            dma((7,)), dma((7,)), dma((3,)), dma((3,)), dma((3,)), dma((3,)), dma((4,)), dma((4,)),
+            dma((7,)), dma((7,)), dma((15,)), dma((15,)), dma, dma,
         ],
-        compiler_params=pltpu.CompilerParams(collective_id=2, has_side_effects=True, vmem_limit_bytes=32 * MIB),
-        name="sums",
-    )(part)
+        compiler_params=pltpu.CompilerParams(collective_id=1, has_side_effects=True, vmem_limit_bytes=60 * MIB),
+        name="gathers",
+    )(right, warm, left, corner, layer)
 
 
 def eliminate(diag):
@@ -539,8 +516,7 @@
     left = jnp.pad(left, ((0, 0), (0, 0), (0, 1), (0, 16))).reshape(392, 128)
     left = jnp.pad(left, ((0, 8), (0, 0)))
     corner = jnp.pad(corner.reshape(112, 32, 14), ((0, 16), (0, 0), (0, 2))).reshape(128, 512)
-    part = gathers(right, warm, left, corner, single_layer.reshape(2, 49, 49))
-    proj, gram = sums(part)
+    proj, gram = gathers(right, warm, left, corner, single_layer.reshape(2, 49, 49))
     r_factor, rows = factor(gram.reshape(4, 512, 128), proj)
     new_basis = rows[:392].reshape(7, 7, 8, 112)[:, :, :7].reshape(7, 49, 112)
     return new_basis, r_factor

time: 187 us -> 177 us (0.947)
  Pallas kernels: 178 us -> 166 us
    pallas_call x2 -> x1, Pallas kernels: 133 us -> 121 us  [gathers(): pl.pallas_call(gather_kernel, out_shape=[jax.ShapeDtypeStruct((4, ROWS, 1...]
    unnamed x11 -> x13, local copies, waits for them, and re-layouts: 2.96 us -> 4.2 us
where the time goes in v3:
time: 177 us; the launch traced here: 176 us
  Pallas kernels  166 us (94%)
  local copies, waits for them, and re-layouts  8.3 us (5%)
    pallas_call x1, Pallas kernels, gathers(): pl.pallas_call(gather_kernel, out_shape=[jax.ShapeDtypeStruct((4, ROWS, 1...  121 us
    pallas_call x1, Pallas kernels, factor(): pl.pallas_call(factor_kernel, out_shape=[jax.ShapeDtypeStruct((448, 448),...  45.2 us
    unnamed x13, local copies, waits for them, and re-layouts  4.2 us

profile of v3, /device:TPU:1, one launch (start us, length us, event | category | flops | bytes accessed | tf_op | source)
XLA Modules:
  0.0 176.4 jit_solution(13404908825053561503)
XLA Ops:
  0.6 0.0 copy-start.5
  0.7 0.7 copy-done.5
  1.3 0.7 reshape.40.layer
  2.1 0.9 reshape.36
  3.1 0.0 copy-start.3
  3.1 0.6 pad.40.left
  3.7 0.3 copy-done.3
  4.0 0.1 reshape.34
  4.1 0.0 copy-start.4
  4.2 0.0 copy-start.2
  4.2 0.9 copy-done.4
  5.1 0.0 copy-done.2
  5.1 0.1 copy.10
  5.3 0.8 copy.11.corner
  6.1 0.9 pad_select_fusion
  7.0 121.3 %gathers.1 = (bf16[4,400,128]{2,1,0:T(8,128)(2,1)}, f32[4,4,2,64,128]{4,3,2,1,0:T(8,128)}) custom-call(bf16[2,16,3200]{2,1,0:T(8,128)(2,1)} %get-tuple-element.11.right, bf16[2,16,3200]{2,1,0:T(8,128)(2,1)} %get-tuple-element.10.warm, bf16[400,128]{1,0:T(8,128)(2,1)} %pad.40.left, bf16[128,512]{1,0:T(8,128)(2,1)} %copy.11.corner, ...), custom_call_target="tpu_custom_call" | custom-call | tf_op jit(solution)/shard_map/gathers/pallas_call | solution.py:397
  128.3 0.0 copy-start
  128.3 1.2 copy-done
  129.5 0.0 copy-start.1
  129.5 1.0 copy-done.1
  130.5 45.2 %factor.1 = (f32[448,448]{1,0:T(8,128)}, f32[400,112]{1,0:T(8,128)S(1)}) custom-call(f32[4,512,128]{2,1,0:T(8,128)S(1)} %bitcast.17, bf16[4,400,128]{2,1,0:T(8,128)(2,1)S(1)} %copy-done.1), custom_call_target="tpu_custom_call" | custom-call | tf_op jit(solution)/shard_map/factor/pallas_call | solution.py:495
  175.7 0.7 reshape.43
  (8 shorter events, 0.2 us)
Async XLA Ops:
  0.6 0.7 copy-start.5
  3.1 0.9 copy-start.3
  4.1 0.9 copy-start.4
  4.2 0.9 copy-start.2
  128.3 1.2 copy-start
  129.5 1.0 copy-start.1

commit v4 on v3

--- a/solution.py
+++ b/solution.py
@@ -432,26 +432,43 @@
 
 def eliminate(diag):
     n = BLOCK
-    row_id = lax.broadcasted_iota(jnp.int32, (n, n), 0)
-    col_id = lax.broadcasted_iota(jnp.int32, (n, n), 1)
-    eye = jnp.where(row_id == col_id, 1.0, 0.0).astype(jnp.float32)
-    wide = jnp.concatenate([diag, eye], axis=1)
+    row_id, col_id = iota((n, n), 0), iota((n, n), 1)
+    wide = jnp.concatenate([diag, jnp.where(row_id == col_id, 1.0, 0.0).astype(jnp.float32)], axis=1)
     groups = [wide[8 * g:8 * g + 8] for g in range(n // 8)]
-    sub = lax.broadcasted_iota(jnp.int32, (8, 2 * n), 0)
-    for k in range(n):
-        g, t = divmod(k, 8)
-        pivot = groups[g][t:t + 1, :]
-        scaled = pivot * (1.0 / pivot[:, k:k + 1])
-        for h in range(g, n // 8):
-            if h == g and t == 7:
-                continue
-            update = groups[h][:, k:k + 1] * scaled
-            if h == g:
-                update = jnp.where(sub > t, update, 0.0)
-            groups[h] = groups[h] - update
+    sub = iota((8, 2 * n), 0)
+
+    def full(v):
+        return jnp.broadcast_to(v, (8, 2 * n))
+
+    for g in range(n // 8):
+        k, own = 8 * g, groups[g]
+        rows = [full(own[i:i + 1, :]) for i in range(8)]
+        cols = [full(own[:, k + j:k + j + 1]) for j in range(8)]
+        e = {(i, j): full(cols[j][i:i + 1, :]) for i in range(8) for j in range(i, 8)}
+        scaled, s = [], {}
+        for r in range(8):
+            inv = 1.0 / e[r, r]
+            scaled.append(rows[r] * inv)
+            for j in range(r + 1, 8):
+                s[r, j] = e[r, j] * inv
+            for i in range(r + 1, 8):
+                rows[i] = rows[i] - e[r, i] * scaled[r]
+                for j in range(i, 8):
+                    e[i, j] = e[i, j] - e[r, i] * s[r, j]
+        for h in range(g + 1, n // 8):
+            below = groups[h]
+            c = [full(below[:, k + j:k + j + 1]) for j in range(8)]
+            for r in range(8):
+                below = below - c[r] * scaled[r]
+                for j in range(r + 1, 8):
+                    c[j] = c[j] - c[r] * s[r, j]
+            groups[h] = below
+        for i in range(1, 8):
+            own = jnp.where(sub == i, rows[i], own)
+        groups[g] = own
     wide = jnp.concatenate(groups, axis=0)
     upper, lower = wide[:, :n], wide[:, n:]
-    d = jnp.sum(upper * eye, axis=1, keepdims=True)
+    d = jnp.sum(jnp.where(row_id == col_id, upper, 0.0), axis=1, keepdims=True)
     root = lax.rsqrt(d)
     root = root * (1.5 - 0.5 * d * root * root)
     return jnp.where(row_id <= col_id, upper * root, 0.0), jnp.where(row_id >= col_id, lower * root, 0.0)

time: 177 us -> 153 us (0.86)
  Pallas kernels: 166 us -> 143 us
    pallas_call x1, Pallas kernels: 45.2 us -> 21.8 us  [factor(): pl.pallas_call(factor_kernel, out_shape=[jax.ShapeDtypeStruct((448, 448),...]
where the time goes in v4:
time: 153 us
  Pallas kernels  143 us (93%)
  local copies, waits for them, and re-layouts  8.3 us (5%)
    pallas_call x1, Pallas kernels, gathers(): pl.pallas_call(gather_kernel, out_shape=[jax.ShapeDtypeStruct((4, ROWS, 1...  121 us
    pallas_call x1, Pallas kernels, factor(): pl.pallas_call(factor_kernel, out_shape=[jax.ShapeDtypeStruct((448, 448),...  21.8 us
    unnamed x13, local copies, waits for them, and re-layouts  4.2 us

profile of v4, /device:TPU:1, one launch (start us, length us, event | category | flops | bytes accessed | tf_op | source)
XLA Modules:
  0.0 153.1 jit_solution(14189538275517592168)
XLA Ops:
  0.6 0.0 copy-start.5
  0.7 0.7 copy-done.5
  1.3 0.7 reshape.40.layer
  2.1 0.9 reshape.36
  3.1 0.0 copy-start.3
  3.1 0.6 pad.40.left
  3.7 0.3 copy-done.3
  4.0 0.1 reshape.34
  4.1 0.0 copy-start.4
  4.2 0.0 copy-start.2
  4.2 0.9 copy-done.4
  5.1 0.0 copy-done.2
  5.1 0.1 copy.10
  5.3 0.8 copy.11.corner
  6.1 0.9 pad_select_fusion
  7.0 121.3 %gathers.1 = (bf16[4,400,128]{2,1,0:T(8,128)(2,1)}, f32[4,4,2,64,128]{4,3,2,1,0:T(8,128)}) custom-call(bf16[2,16,3200]{2,1,0:T(8,128)(2,1)} %get-tuple-element.11.right, bf16[2,16,3200]{2,1,0:T(8,128)(2,1)} %get-tuple-element.10.warm, bf16[400,128]{1,0:T(8,128)(2,1)} %pad.40.left, bf16[128,512]{1,0:T(8,128)(2,1)} %copy.11.corner, ...), custom_call_target="tpu_custom_call" | custom-call | tf_op jit(solution)/shard_map/gathers/pallas_call | solution.py:397
  128.3 0.0 copy-start
  128.3 1.2 copy-done
  129.5 0.0 copy-start.1
  129.5 1.0 copy-done.1
  130.5 21.8 %factor.1 = (f32[448,448]{1,0:T(8,128)}, f32[400,112]{1,0:T(8,128)S(1)}) custom-call(f32[4,512,128]{2,1,0:T(8,128)S(1)} %bitcast.17, bf16[4,400,128]{2,1,0:T(8,128)(2,1)S(1)} %copy-done.1), custom_call_target="tpu_custom_call" | custom-call | tf_op jit(solution)/shard_map/factor/pallas_call | solution.py:512
  152.4 0.7 reshape.43
  (8 shorter events, 0.2 us)
Async XLA Ops:
  0.6 0.7 copy-start.5
  3.1 0.9 copy-start.3
  4.1 0.9 copy-start.4
  4.2 0.9 copy-start.2
  128.3 1.2 copy-start
  129.5 1.0 copy-start.1

commit v5 on v4

--- a/solution.py
+++ b/solution.py
@@ -135,13 +135,12 @@
         forward_partner(g, 0, y, z, a)
         forward_partner(g, 1, y, z, b)
 
-    def column(g):
-        for d in (1, 2, 3):
-            yy = ymove(d)
-            arrived(g, 0, yy, z)
-            send(g, 0, yy, z, znext)
-            send(g, 0, yy, z, zprev)
-            forward_partner(g, 0, yy, z)
+    def column(g, d):
+        yy = ymove(d)
+        arrived(g, 0, yy, z)
+        send(g, 0, yy, z, znext)
+        send(g, 0, yy, z, zprev)
+        forward_partner(g, 0, yy, z)
 
     def b_ring(g, s, way):
         zz = zmove(-s) if way > 0 else zmove(s)
@@ -176,18 +175,45 @@
         forward_partner(g, 1, ymove(2), zz)
 
     def ring_steps(g):
-        steps = [lambda: y_pass(g, z)]
-        for k in (1, 2, 3, 4):
-            for way in (1, -1):
-                if way < 0 and k == 4:
-                    continue
-                steps.append(functools.partial(b_ring, g, k, way))
-                steps.extend(functools.partial(a_ring, g, k, way, d) for d in range(4))
-            if k > 1:
-                steps.append(functools.partial(y_pass, g, zmove(-(k - 1))))
-                steps.append(functools.partial(y_pass, g, zmove(k - 1)))
-        steps.append(lambda: y_pass(g, zmove(-4)))
-        steps.extend(functools.partial(y_last, g, zmove(k)) for k in range(8))
+        steps = []
+
+        def b_hop(k):
+            steps.append(functools.partial(b_ring, g, k, 1))
+            if k < 4:
+                steps.append(functools.partial(b_ring, g, k, -1))
+
+        def a_hop(k):
+            for d in range(4):
+                steps.append(functools.partial(a_ring, g, k, 1, d))
+                if k < 4:
+                    steps.append(functools.partial(a_ring, g, k, -1, d))
+
+        def y_hop(k):
+            steps.append(functools.partial(y_pass, g, zmove(-k)))
+            if 0 < k < 4:
+                steps.append(functools.partial(y_pass, g, zmove(k)))
+
+        def y_end(*ks):
+            steps.extend(functools.partial(y_last, g, zmove(k)) for k in ks)
+
+        b_hop(1)
+        steps.extend(functools.partial(column, g, d) for d in (1, 3, 2))
+        y_hop(0)
+        b_hop(2)
+        y_hop(1)
+        a_hop(1)
+        b_hop(3)
+        y_hop(2)
+        b_hop(4)
+        y_end(0)
+        a_hop(2)
+        y_hop(3)
+        y_end(-1, 1)
+        y_hop(4)
+        y_end(-2, 2)
+        a_hop(3)
+        y_end(-3, 3, 4)
+        a_hop(4)
         return steps
 
     def from_partner(g):
@@ -198,20 +224,18 @@
 
     begin(0)
     weights(layer, ket, bra)
-    column(0)
     steps = ring_steps(0)
-    for step in steps[:-17]:
+    for step in steps[:-8]:
         step()
-    begin(1)
-    for step in steps[-17:]:
-        step()
-    column(1)
     for c in xcopies + own_x:
         c.wait()
     acc = jnp.zeros((ROWS, 512), jnp.float32)
     for n in range(4):
         acc += jnp.dot(left_all[n], corner_all[n], preferred_element_type=jnp.float32)
     half[...] = acc.astype(jnp.bfloat16)
+    begin(1)
+    for step in steps[-8:]:
+        step()
     own_copies[0].wait()
     from_partner(0)
 
@@ -220,7 +244,7 @@
     done = 0
     for k, compute in enumerate(work):
         compute()
-        upto = len(steps) * (k + 1) // len(work)
+        upto = int(len(steps) * ((k + 1) / len(work)) ** 1.5)
         for step in steps[done:upto]:
             step()
         done = upto
@@ -425,7 +449,7 @@
             dma((3,)), dma((3,)), dma((3,)), dma((3,)), dma((7,)), dma((7,)), dma((7,)), dma((7,)),
             dma((7,)), dma((7,)), dma((15,)), dma((15,)), dma, dma,
         ],
-        compiler_params=pltpu.CompilerParams(collective_id=1, has_side_effects=True, vmem_limit_bytes=60 * MIB),
+        compiler_params=pltpu.CompilerParams(collective_id=1, has_side_effects=True, vmem_limit_bytes=46 * MIB),
         name="gathers",
     )(right, warm, left, corner, layer)
 

time: 153 us -> 138 us (0.902)
  Pallas kernels: 143 us -> 132 us
  local copies, waits for them, and re-layouts: 8.3 us -> 4.79 us
    pallas_call x1, Pallas kernels: 121 us -> 110 us  [gathers(): pl.pallas_call(gather_kernel, out_shape=[jax.ShapeDtypeStruct((4, ROWS, 1...]
    unnamed x13 -> x9, local copies, waits for them, and re-layouts: 4.2 us -> 2.58 us
where the time goes in v5:
time: 138 us; the launch traced here: 137 us
  Pallas kernels  132 us (96%)
  local copies, waits for them, and re-layouts  4.79 us (3%)
    pallas_call x1, Pallas kernels, gathers(): pl.pallas_call(gather_kernel, out_shape=[jax.ShapeDtypeStruct((4, ROWS, 1...  110 us
    pallas_call x1, Pallas kernels, factor(): pl.pallas_call(factor_kernel, out_shape=[jax.ShapeDtypeStruct((448, 448),...  21.8 us

profile of v5, /device:TPU:1, one launch (start us, length us, event | category | flops | bytes accessed | tf_op | source)
XLA Modules:
  0.0 137.4 jit_solution(14434790212016588616)
XLA Ops:
  0.6 0.0 copy-start.3
  0.7 0.7 copy-done.3
  1.3 0.1 reshape.40.layer
  1.5 0.9 reshape.36
  2.5 0.0 copy-start.1
  2.5 0.9 copy-done.1
  3.4 0.1 reshape.34
  3.5 0.0 copy-start.2
  3.6 0.0 copy-start
  3.6 0.9 copy-done.2
  4.5 0.0 copy-done
  4.5 0.1 copy.10
  4.7 0.1 copy.11.corner
  4.8 0.1 pad_select_fusion
  5.0 109.9 %gathers.1 = (bf16[4,400,128]{2,1,0:T(8,128)(2,1)S(1)}, f32[4,4,2,64,128]{4,3,2,1,0:T(8,128)S(1)}) custom-call(bf16[2,16,3200]{2,1,0:T(8,128)(2,1)S(1)} %get-tuple-element.11.right, bf16[2,16,3200]{2,1,0:T(8,128)(2,1)S(1)} %get-tuple-element.10.warm, bf16[400,128]{1,0:T(8,128)(2,1)S(1)} %pad.40.left, bf16[128,512]{1,0:T(8,128)(2,1)S(1)} %copy.11.corner, ...), custom_call_target="tpu_custom_call" | custom-call | tf_op jit(solution)/shard_map/gathers/pallas_call | solution.py:421
  114.9 21.8 %factor.1 = (f32[448,448]{1,0:T(8,128)}, f32[400,112]{1,0:T(8,128)S(1)}) custom-call(f32[4,512,128]{2,1,0:T(8,128)S(1)} %bitcast.17, bf16[4,400,128]{2,1,0:T(8,128)(2,1)S(1)} %get-tuple-element.7.proj), custom_call_target="tpu_custom_call" | custom-call | tf_op jit(solution)/shard_map/factor/pallas_call | solution.py:536
  136.7 0.7 reshape.43
  (9 shorter events, 0.2 us)
Async XLA Ops:
  0.6 0.7 copy-start.3
  2.5 0.9 copy-start.1
  3.5 0.9 copy-start.2
  3.6 0.9 copy-start

commit v6 on v5

--- a/solution.py
+++ b/solution.py
@@ -275,8 +275,8 @@
     scale = 1.0 / (448 * 49)
 
     def product(n):
-        slab[pl.ds(pl.multiple_of(n * 128, 128), 128), :] = lax.dot_general(
-            proj[n], own, tn, preferred_element_type=jnp.float32) * scale
+        full = lax.dot_general(proj[n], own, tn, preferred_element_type=jnp.float32) * scale
+        slab[pl.ds(pl.multiple_of(n * 112, 112), 112), :] = full[0:112]
 
     product(x)
     for d in (0, 2, 1):
@@ -287,13 +287,14 @@
         return pl.ds(pl.multiple_of(k * size, size), size)
 
     mine = y * 2 + core
-    c3 = [start(slab.at[rows(yy * 2 + cc, 64)], got1.at[k], a_s.at[k], a_r.at[k], (wide_of(yy, z, cc), x))
+    c3 = [start(slab.at[rows(yy * 2 + cc, 56)], got1.at[k], a_s.at[k], a_r.at[k], (wide_of(yy, z, cc), x))
           for k, (yy, cc) in enumerate(others)]
-    acc = slab[rows(mine, 64), :]
+    acc = slab[rows(mine, 56), :]
     for k in range(7):
         c3[k].wait_recv()
         acc += got1[k]
-    piece[...] = acc
+    piece[0:56, :] = acc
+    piece[56:64, :] = jnp.zeros((8, 128), jnp.float32)
     c4 = [start(piece.at[rows(zz, 8)], got2.at[k], b_s.at[k], b_r.at[k], (wide_of(y, zz, core), x))
           for k, zz in enumerate(zs)]
     acc = piece[rows(z, 8), :]
@@ -305,16 +306,16 @@
     c5 = [start(spot, spot, c_s.at[k], c_r.at[k], at(y, zz)) for k, zz in enumerate(zs)]
     for c in c5:
         c.wait_recv()
-    spot = gram.at[x, y, core]
+    spot = gram.at[x, y, core, 0:56]
     c6 = [start(spot, spot, d_s.at[k], d_r.at[k], (wide_of(yy, z, core), xx)) for k, (xx, yy) in enumerate(plane)]
     start(spot, spot, f_s, f_r, partner)
     for k in (7, 8, 9, 10, 2, 1, 11, 12, 13, 14, 3, 4, 5, 6, 0):
         xx, yy = plane[k]
         c6[k].wait_recv()
-        spot = gram.at[lax.rem(2 * x + 4 - xx, 4), lax.rem(2 * y + 4 - yy, 4), core]
+        spot = gram.at[lax.rem(2 * x + 4 - xx, 4), lax.rem(2 * y + 4 - yy, 4), core, 0:56]
         start(spot, spot, f_s, f_r, partner)
-    settle(gram.at[:, :, core], f_s)
-    settle(gram.at[:, :, 1 - core], f_r)
+    settle(gram.at[:, :, core, 0:56], f_s)
+    settle(gram.at[:, :, 1 - core, 0:56], f_r)
     for c in c1 + c2 + c3 + c4 + c5 + c6:
         c.wait_send()
     for g in (0, 1):
@@ -441,8 +442,8 @@
             pltpu.VMEM((2, SLOT, HALF), jnp.bfloat16),
             pltpu.VMEM((4, ROWS, 128), jnp.bfloat16),
             pltpu.VMEM((3, ROWS, 128), jnp.bfloat16),
-            pltpu.VMEM((512, 128), jnp.float32),
-            pltpu.VMEM((7, 64, 128), jnp.float32),
+            pltpu.VMEM((448, 128), jnp.float32),
+            pltpu.VMEM((7, 56, 128), jnp.float32),
             pltpu.VMEM((64, 128), jnp.float32),
             pltpu.VMEM((7, 8, 128), jnp.float32),
             dma((2,)), dma((2,)), dma((4,)), dma((2, 2, 32)), dma((2,)), dma((2,)), dma((2,)), dma((2, 3)), dma((2, 3)),
@@ -503,13 +504,20 @@
     x = lax.axis_index("narrow")
     for a in range(4):
         for b in range(4):
-            work[a * 112:(a + 1) * 112, b * 112:(b + 1) * 112] = gram[b, a * 128:a * 128 + 112, 0:112]
+            for c in range(2):
+                first = a * 112 + c * 56
+                work[first:first + 56, b * 112:(b + 1) * 112] = gram[b, a, c, 0:56, 0:112]
     r_ref[...] = jnp.zeros_like(r_ref)
     col = lax.broadcasted_iota(jnp.int32, (BLOCK, n), 1)
     row = lax.broadcasted_iota(jnp.int32, (BLOCK, n), 0)
+    ahead = work[0:BLOCK, 0:BLOCK]
     for b in range(n // BLOCK):
         lo, hi = b * BLOCK, (b + 1) * BLOCK
-        r, inverse = eliminate(work[lo:hi, lo:hi])
+        r, inverse = eliminate(ahead)
+        if hi < n:
+            near = jnp.dot(inverse, work[lo:hi, hi:hi + BLOCK], precision=HI, preferred_element_type=jnp.float32)
+            ahead = work[hi:hi + BLOCK, hi:hi + BLOCK] - lax.dot_general(
+                near, near, (((0,), (0,)), ((), ())), precision=HI, preferred_element_type=jnp.float32)
         inside = (col >= lo) & (col < hi)
         src = jnp.where(inside, jnp.where(col - lo == row, 1.0, 0.0), work[lo:hi, :])
         full = jnp.dot(inverse, src, precision=HI, preferred_element_type=jnp.float32)
@@ -558,7 +566,7 @@
     left = jnp.pad(left, ((0, 8), (0, 0)))
     corner = jnp.pad(corner.reshape(112, 32, 14), ((0, 16), (0, 0), (0, 2))).reshape(128, 512)
     proj, gram = gathers(right, warm, left, corner, single_layer.reshape(2, 49, 49))
-    r_factor, rows = factor(gram.reshape(4, 512, 128), proj)
+    r_factor, rows = factor(gram, proj)
     new_basis = rows[:392].reshape(7, 7, 8, 112)[:, :, :7].reshape(7, 49, 112)
     return new_basis, r_factor
 

time: 138 us -> 136 us (0.986)
  Pallas kernels: 132 us -> 130 us
where the time goes in v6:
time: 136 us
  Pallas kernels  130 us (96%)
  local copies, waits for them, and re-layouts  4.79 us (4%)
    pallas_call x1, Pallas kernels, gathers(): pl.pallas_call(gather_kernel, out_shape=[jax.ShapeDtypeStruct((4, ROWS, 1...  109 us
    pallas_call x1, Pallas kernels, factor(): pl.pallas_call(factor_kernel, out_shape=[jax.ShapeDtypeStruct((448, 448),...  21 us

profile of v6, /device:TPU:1, one launch (start us, length us, event | category | flops | bytes accessed | tf_op | source)
XLA Modules:
  0.0 135.7 jit_solution(5661722463801713169)
XLA Ops:
  0.6 0.0 copy-start.3
  0.7 0.7 copy-done.3
  1.3 0.1 reshape.37.layer
  1.5 0.9 reshape.33
  2.5 0.0 copy-start.1
  2.5 0.9 copy-done.1
  3.4 0.1 reshape.31
  3.5 0.0 copy-start.2
  3.6 0.0 copy-start
  3.6 0.9 copy-done.2
  4.5 0.0 copy-done
  4.5 0.1 copy.10
  4.7 0.1 copy.11.corner
  4.8 0.1 pad_select_fusion
  5.0 109.1 %gathers.1 = (bf16[4,400,128]{2,1,0:T(8,128)(2,1)S(1)}, f32[4,4,2,64,128]{4,3,2,1,0:T(8,128)S(1)}) custom-call(bf16[2,16,3200]{2,1,0:T(8,128)(2,1)S(1)} %get-tuple-element.11.right, bf16[2,16,3200]{2,1,0:T(8,128)(2,1)S(1)} %get-tuple-element.10.warm, bf16[400,128]{1,0:T(8,128)(2,1)S(1)} %pad.40.left, bf16[128,512]{1,0:T(8,128)(2,1)S(1)} %copy.11.corner, ...), custom_call_target="tpu_custom_call" | custom-call | tf_op jit(solution)/shard_map/gathers/pallas_call | solution.py:422
  114.0 21.0 %factor.1 = (f32[448,448]{1,0:T(8,128)}, f32[400,112]{1,0:T(8,128)S(1)}) custom-call(f32[4,4,2,64,128]{4,3,2,1,0:T(8,128)S(1)} %get-tuple-element.6.gram, bf16[4,400,128]{2,1,0:T(8,128)(2,1)S(1)} %get-tuple-element.7.proj), custom_call_target="tpu_custom_call" | custom-call | tf_op jit(solution)/shard_map/factor/pallas_call | solution.py:544
  135.0 0.7 reshape.39
  (9 shorter events, 0.2 us)
Async XLA Ops:
  0.6 0.7 copy-start.3
  2.5 0.9 copy-start.1
  3.5 0.9 copy-start.2
  3.6 0.9 copy-start

commit v7 on v6

--- a/solution.py
+++ b/solution.py
@@ -531,11 +531,16 @@
             work[hi:, :] = old - lax.dot_general(rest[:, hi:], full, (((0,), (0,)), ((), ())), precision=HI,
                                                  preferred_element_type=jnp.float32)
     own = work[pl.ds(pl.multiple_of(x * 112, 8), 112), :]
+    high = own.astype(jnp.bfloat16)
+    rest = own - high.astype(jnp.float32)
+    mid = rest.astype(jnp.bfloat16)
+    low = (rest - mid.astype(jnp.float32)).astype(jnp.bfloat16)
     nt = (((1,), (1,)), ((), ()))
     acc = jnp.zeros((ROWS, 112), jnp.float32)
     for b in range(4):
-        acc += lax.dot_general(proj[b][:, 0:112].astype(jnp.float32), own[:, b * 112:(b + 1) * 112], nt, precision=HI,
-                               preferred_element_type=jnp.float32)
+        for piece in (low, mid, high):
+            acc += lax.dot_general(proj[b][:, 0:112], piece[:, b * 112:(b + 1) * 112], nt,
+                                   preferred_element_type=jnp.float32)
     out[...] = acc
 
 

time: 136 us -> 135 us (level)
  no operation moved by 1% of the time
where the time goes in v7:
time: 135 us
  Pallas kernels  129 us (96%)
  local copies, waits for them, and re-layouts  4.79 us (4%)
    pallas_call x1, Pallas kernels, gathers(): pl.pallas_call(gather_kernel, out_shape=[jax.ShapeDtypeStruct((4, ROWS, 1...  109 us
    pallas_call x1, Pallas kernels, factor(): pl.pallas_call(factor_kernel, out_shape=[jax.ShapeDtypeStruct((448, 448),...  20.2 us

profile of v7, /device:TPU:1, one launch (start us, length us, event | category | flops | bytes accessed | tf_op | source)
XLA Modules:
  0.0 135.0 jit_solution(11779880853837134606)
XLA Ops:
  0.6 0.0 copy-start.3
  0.7 0.7 copy-done.3
  1.3 0.1 reshape.37.layer
  1.5 0.9 reshape.33
  2.5 0.0 copy-start.1
  2.5 0.9 copy-done.1
  3.4 0.1 reshape.31
  3.5 0.0 copy-start.2
  3.6 0.0 copy-start
  3.6 0.9 copy-done.2
  4.5 0.0 copy-done
  4.5 0.1 copy.10
  4.7 0.1 copy.11.corner
  4.8 0.1 pad_select_fusion
  5.0 109.1 %gathers.1 = (bf16[4,400,128]{2,1,0:T(8,128)(2,1)S(1)}, f32[4,4,2,64,128]{4,3,2,1,0:T(8,128)S(1)}) custom-call(bf16[2,16,3200]{2,1,0:T(8,128)(2,1)S(1)} %get-tuple-element.11.right, bf16[2,16,3200]{2,1,0:T(8,128)(2,1)S(1)} %get-tuple-element.10.warm, bf16[400,128]{1,0:T(8,128)(2,1)S(1)} %pad.40.left, bf16[128,512]{1,0:T(8,128)(2,1)S(1)} %copy.11.corner, ...), custom_call_target="tpu_custom_call" | custom-call | tf_op jit(solution)/shard_map/gathers/pallas_call | solution.py:422
  114.0 20.2 %factor.1 = (f32[448,448]{1,0:T(8,128)}, f32[400,112]{1,0:T(8,128)S(1)}) custom-call(f32[4,4,2,64,128]{4,3,2,1,0:T(8,128)S(1)} %get-tuple-element.6.gram, bf16[4,400,128]{2,1,0:T(8,128)(2,1)S(1)} %get-tuple-element.7.proj), custom_call_target="tpu_custom_call" | custom-call | tf_op jit(solution)/shard_map/factor/pallas_call | solution.py:549
  134.3 0.7 reshape.39
  (9 shorter events, 0.2 us)
Async XLA Ops:
  0.6 0.7 copy-start.3
  2.5 0.9 copy-start.1
  3.5 0.9 copy-start.2
  3.6 0.9 copy-start
